TPU v7x, 256 devices: a whole 4x4x8 slice. The times are simulated.
256 devices in a mesh: gx: 4 (over y), gy: 8 (over z), gz: 8 (over x, core).
Axes of the slice: x: 4, y: 4, z: 8, core: 2. Of those that a mesh axis runs over, the one named last changes fastest.
Arguments:
- rhs: float32 [64, 384, 1024], P('gx', 'gy', 'gz'), may hold values from -6000 to 6000
- coef_b: float32 [64, 384, 1024], P('gx', 'gy', 'gz'), may hold values from 1 to 10
- coef_c: float32 [64, 384, 1024], P('gx', 'gy', 'gz'), may hold values from 1 to 10
Outputs:
- solution: float32 [64, 384, 1024], P('gx', 'gy', 'gz')
All inputs are finite; a program needn't handle non-finite values.
Results may differ from a plain program's by a relative error of at most 0.0001.
Values sent between devices are 32-bit elements; how exact they have to be, the bound alone decides.
A program may use at most 128 MiB of HBM per device.

v0:
```python
import jax
import jax.numpy as jnp
from jax import lax
from jax.sharding import PartitionSpec as P

LEVELS = 4
SWEEPS = 2
COARSE_SWEEPS = 6


CENTRE = 1.1
RADIUS = 0.9


def padded_2(value, sides, width):
    for axis, dim in sides:
        count, length = (lax.axis_size(axis), value.shape[dim])
        up = [(i, (i + 1) % count) for i in range(count - 1)]
        down = [(j, i) for i, j in up]
        last = lax.slice_in_dim(value, length - width, length, axis=dim)
        initial = lax.slice_in_dim(value, 0, width, axis=dim)
        before = lax.ppermute(last, axis, up)
        after = lax.ppermute(initial, axis, down)
        value = jnp.concatenate([before, value, after], axis=dim)
    return value


def neighbours(padded):
    return (
        padded[:-2, 1:-1, 1:-1],
        padded[2:, 1:-1, 1:-1],
        padded[1:-1, :-2, 1:-1],
        padded[1:-1, 2:, 1:-1],
        padded[1:-1, 1:-1, :-2],
        padded[1:-1, 1:-1, 2:],
    )


def faces_of(coef_pad):
    middle = coef_pad[1:-1, 1:-1, 1:-1]
    return tuple((0.5 * (middle + other) for other in neighbours(coef_pad)))


def diagonal_of(face_terms, cell_term, level_scale):
    summed = (
        face_terms[0]
        + face_terms[1]
        + face_terms[2]
        + face_terms[3]
        + face_terms[4]
        + face_terms[5]
    )
    return cell_term + level_scale * summed


def operator(padded, face_terms, cell_term, level_scale):
    middle = padded[1:-1, 1:-1, 1:-1]
    beside = neighbours(padded)
    summed = face_terms[0] * (middle - beside[0])
    for position in range(1, 6):
        summed = summed + face_terms[position] * (middle - beside[position])
    return cell_term * middle + level_scale * summed


def coarsen(values):
    shape = values.shape
    return values.reshape(shape[0] // 2, 2, shape[1] // 2, 2, shape[2] // 2, 2).mean(axis=(1, 3, 5))


def refine(values):
    return jnp.repeat(jnp.repeat(jnp.repeat(values, 2, axis=0), 2, axis=1), 2, axis=2)


def smooth(approx, source, face_terms, cell_term, level_scale, diagonal, sweeps, padder, from_zero):
    if from_zero:
        remain = source
    else:
        remain = source - operator(padder(approx), face_terms, cell_term, level_scale)
    update = remain / (CENTRE * diagonal)
    approx = update if from_zero else approx + update
    ratio_now = RADIUS / CENTRE
    for sweep_index in range(sweeps - 1):
        remain = source - operator(padder(approx), face_terms, cell_term, level_scale)
        ratio_next = 1.0 / (2.0 * CENTRE / RADIUS - ratio_now)
        update = ratio_next * ratio_now * update + 2.0 * ratio_next / RADIUS * remain / diagonal
        approx = approx + update
        ratio_now = ratio_next
    return approx


def cell_rim(values):
    return padded_2(values, (("gx", 0), ("gy", 1), ("gz", 2)), 1)


def flat_rim(values):
    return padded_2(values, (("gx", 0), ("gy", 1), ("gz", 2)), 1)


def local(rhs, coef_b, coef_c):
    source = rhs
    coef_now = coef_b
    cell_term = coef_c
    saved = []
    for level_index in range(LEVELS - 1):
        level_scale = 4.0 ** (LEVELS - 1 - level_index)
        coef_pad = padded_2(coef_now, (("gx", 0), ("gy", 1), ("gz", 2)), 1)
        face_terms = faces_of(coef_pad)
        diagonal = diagonal_of(face_terms, cell_term, level_scale)
        approx = smooth(
            None, source, face_terms, cell_term, level_scale, diagonal, SWEEPS, cell_rim, True
        )
        remain = source - operator(cell_rim(approx), face_terms, cell_term, level_scale)
        saved.append((approx, source, face_terms, cell_term, level_scale, diagonal))
        source = coarsen(remain)
        coef_now = coarsen(coef_pad[1:-1, 1:-1, 1:-1])
        cell_term = coarsen(cell_term)
    level_scale = 1.0
    coef_pad = padded_2(coef_now, (("gx", 0), ("gy", 1), ("gz", 2)), 1)
    face_terms = faces_of(coef_pad)
    diagonal = diagonal_of(face_terms, cell_term, level_scale)
    coarse = smooth(
        None, source, face_terms, cell_term, level_scale, diagonal, COARSE_SWEEPS, flat_rim, True
    )
    for level_index in range(LEVELS - 2, -1, -1):
        approx, source, face_terms, cell_term, level_scale, diagonal = saved[level_index]
        approx = approx + refine(coarse)
        coarse = smooth(
            approx, source, face_terms, cell_term, level_scale, diagonal, SWEEPS, cell_rim, False
        )
    return coarse


def solution(mesh):
    return jax.shard_map(
        local,
        mesh=mesh,
        in_specs=(P("gx", "gy", "gz"), P("gx", "gy", "gz"), P("gx", "gy", "gz")),
        out_specs=P("gx", "gy", "gz"),
        check_vma=False,
    )
```

profile of v0, /device:TPU:1, one launch (start us, length us, event | category | flops | bytes accessed | tf_op | source)
XLA Modules:
  0.0 681.6 jit_solution(8507299584892431357)
XLA Ops:
  0.8 4.0 collective-permute-start
  10.7 4.2 collective-permute-start.2
  15.9 5.0 collective-permute-start.5
  23.9 4.8 collective-permute-done.5
  36.7 27.2 %reshape.60 = f32[8,2,24,2,64,2]{5,4,3,2,1,0:T(8,128)} reshape(f32[16,48,128]{2,1,0:T(8,128)} %param.4) | data formatting | bytes 786432 | tf_op jit(solution)/shard_map/reshape | solution.py:67
  63.9 9.4 %reduce_sum.83 = f32[8,24,64]{2,1,0:T(8,128)S(1)} reduce(f32[8,2,24,2,64,2]{5,4,3,2,1,0:T(8,128)} %reshape.60, f32[]{:T(128)} %constant.22.clone.1), dimensions={1,3,5}, to_apply=%region_2.0 | reduce | flops 86016 | bytes 442372 | tf_op jit(solution)/shard_map/reduce_sum | solution.py:67
  83.1 5.9 collective-permute-start.10
  92.9 5.0 collective-permute-start.18
  97.9 26.5 %reshape.59 = f32[8,2,24,2,64,2]{5,4,3,2,1,0:T(8,128)} reshape(f32[16,48,128]{2,1,0:T(8,128)S(1)} %copy-done.1) | data formatting | bytes 786432 | tf_op jit(solution)/shard_map/reshape | solution.py:67
  124.4 5.0 div.99
  129.3 9.4 %reduce_sum.82 = f32[8,24,64]{2,1,0:T(8,128)S(1)} reduce(f32[8,2,24,2,64,2]{5,4,3,2,1,0:T(8,128)} %reshape.59, f32[]{:T(128)} %constant.22.clone.1), dimensions={1,3,5}, to_apply=%region_1.0 | reduce | flops 86016 | bytes 442372 | tf_op jit(solution)/shard_map/reduce_sum | solution.py:67
  150.2 4.9 collective-permute-start.20
  155.2 5.1 collective-permute-start.14
  161.7 4.5 collective-permute-done.15
  166.5 5.9 collective-permute-start.16
  184.1 27.2 %reshape.58 = f32[8,2,24,2,64,2]{5,4,3,2,1,0:T(8,128)} reshape(f32[16,48,128]{2,1,0:T(8,128)} %fusion.50) | data formatting | bytes 786432 | tf_op jit(solution)/shard_map/reshape | solution.py:67
  211.4 9.4 %reduce_sum.81 = f32[8,24,64]{2,1,0:T(8,128)S(1)} reduce(f32[8,2,24,2,64,2]{5,4,3,2,1,0:T(8,128)} %reshape.58, f32[]{:T(128)} %constant.22.clone.1), dimensions={1,3,5}, to_apply=%region_0.0 | reduce | flops 86016 | bytes 442372 | tf_op jit(solution)/shard_map/reduce_sum | solution.py:67
  222.7 4.3 collective-permute-start.24
  231.4 4.8 collective-permute-start.26
  244.3 4.0 collective-permute-start.28
  251.5 5.1 div.97
  269.7 4.9 collective-permute-start.38
  282.8 5.6 collective-permute-start.34
  298.5 5.1 reshape.61
  307.4 4.3 collective-permute-start.42
  316.1 4.1 collective-permute-start.44
  326.2 4.3 collective-permute-start.46
  345.1 4.9 collective-permute-start.56
  358.2 5.6 collective-permute-start.52
  378.2 4.3 collective-permute-start.60
  386.8 4.1 collective-permute-start.62
  395.8 5.0 collective-permute-start.64
  420.7 4.8 collective-permute-start.70
  445.3 4.8 collective-permute-start.76
  469.3 4.8 collective-permute-start.82
  493.3 4.8 collective-permute-start.88
  523.1 4.8 collective-permute-start.94
  547.8 4.6 collective-permute-start.100
  576.8 4.6 collective-permute-start.106
  583.6 4.4 collective-permute-done.107
  602.7 4.6 collective-permute-start.112
  609.5 4.4 collective-permute-done.113
  634.0 4.6 collective-permute-start.118
  640.5 4.1 collective-permute-done.118
  644.6 4.4 collective-permute-done.119
  664.5 4.4 collective-permute-start.124
  670.8 4.1 collective-permute-done.124
  674.9 4.4 collective-permute-done.125
  (412 shorter events, 372.9 us)
Async XLA Ops:
  15.9 12.8 %collective-permute-start.5 = (f32[18,50,1]{2,1,0:T(8,128)S(1)}, f32[18,50,1]{2,1,0:T(8,128)S(1)}, u32[]{:S(2)}, u32[]{:S(2)}) collective-permute-start(f32[18,50,1]{2,1,0:T(8,128)S(1)} %get-tuple-element.47), channel_id=1, source_target_pairs={{1,0},{2,1},{3,2},{4,3},{5,4},{6,5},{7,6},{9,8},{10,9},{11,10},{12... | collective-permute-start | bytes 10808 | tf_op jit(solution)/shard_map/ppermute | solution.py:23
  20.9 9.0 %collective-permute-start.4 = (f32[18,50,1]{2,1,0:T(8,128)S(1)}, f32[18,50,1]{2,1,0:T(8,128)S(1)}, u32[]{:S(2)}, u32[]{:S(2)}) collective-permute-start(f32[18,50,1]{2,1,0:T(8,128)S(1)} %get-tuple-element.48), channel_id=1, source_target_pairs={{0,1},{1,2},{2,3},{3,4},{4,5},{5,6},{6,7},{8,9},{9,10},{10,11},{11... | collective-permute-start | bytes 10808 | tf_op jit(solution)/shard_map/ppermute | solution.py:22
  32.0 41.3 %collective-permute-start.6 = (f32[1,48,128]{2,1,0:T(8,128)S(1)}, f32[1,48,128]{2,1,0:T(8,128)S(1)}, u32[]{:S(2)}, u32[]{:S(2)}) collective-permute-start(f32[1,48,128]{2,1,0:T(8,128)S(1)} %get-tuple-element.65), channel_id=1, source_target_pairs={{0,64},{64,128},{128,192},{1,65},{65,129},{129,193},{2,66},{66,130... | collective-permute-start | bytes 73736 | tf_op jit(solution)/shard_map/ppermute | solution.py:22
  35.3 38.1 %collective-permute-start.7 = (f32[1,48,128]{2,1,0:T(8,128)S(1)}, f32[1,48,128]{2,1,0:T(8,128)S(1)}, u32[]{:S(2)}, u32[]{:S(2)}) collective-permute-start(f32[1,48,128]{2,1,0:T(8,128)S(1)} %get-tuple-element.66), channel_id=1, source_target_pairs={{64,0},{128,64},{192,128},{65,1},{129,65},{193,129},{66,2},{130,66... | collective-permute-start | bytes 73736 | tf_op jit(solution)/shard_map/ppermute | solution.py:23
  83.1 57.9 %collective-permute-start.10 = (f32[18,50,1]{2,1,0:T(8,128)}, f32[18,50,1]{2,1,0:T(8,128)}, u32[]{:S(2)}, u32[]{:S(2)}) collective-permute-start(f32[18,50,1]{2,1,0:T(8,128)} %get-tuple-element.45), channel_id=1, source_target_pairs={{0,1},{1,2},{2,3},{3,4},{4,5},{5,6},{6,7},{8,9},{9,10},{10,11},{11... | collective-permute-start | bytes 10808 | tf_op jit(solution)/shard_map/ppermute | solution.py:22
  89.0 52.0 %collective-permute-start.11 = (f32[18,50,1]{2,1,0:T(8,128)}, f32[18,50,1]{2,1,0:T(8,128)}, u32[]{:S(2)}, u32[]{:S(2)}) collective-permute-start(f32[18,50,1]{2,1,0:T(8,128)} %get-tuple-element.46), channel_id=1, source_target_pairs={{1,0},{2,1},{3,2},{4,3},{5,4},{6,5},{7,6},{9,8},{10,9},{11,10},{12... | collective-permute-start | bytes 10808 | tf_op jit(solution)/shard_map/ppermute | solution.py:23
  91.5 57.3 %collective-permute-start.19 = (f32[1,24,64]{2,1,0:T(8,128)}, f32[1,24,64]{2,1,0:T(8,128)S(1)}, u32[]{:S(2)}, u32[]{:S(2)}) collective-permute-start(f32[1,24,64]{2,1,0:T(8,128)} %get-tuple-element.97), channel_id=1, source_target_pairs={{64,0},{128,64},{192,128},{65,1},{129,65},{193,129},{66,2},{130,66... | collective-permute-start | bytes 18440 | tf_op jit(solution)/shard_map/ppermute | solution.py:23
  92.9 56.0 %collective-permute-start.18 = (f32[1,24,64]{2,1,0:T(8,128)}, f32[1,24,64]{2,1,0:T(8,128)S(1)}, u32[]{:S(2)}, u32[]{:S(2)}) collective-permute-start(f32[1,24,64]{2,1,0:T(8,128)} %get-tuple-element.98), channel_id=1, source_target_pairs={{0,64},{64,128},{128,192},{1,65},{65,129},{129,193},{2,66},{66,130... | collective-permute-start | bytes 18440 | tf_op jit(solution)/shard_map/ppermute | solution.py:22
  144.2 11.0 %collective-permute-start.12 = (f32[1,48,128]{2,1,0:T(8,128)S(1)}, f32[1,48,128]{2,1,0:T(8,128)S(1)}, u32[]{:S(2)}, u32[]{:S(2)}) collective-permute-start(f32[1,48,128]{2,1,0:T(8,128)S(1)} %get-tuple-element.63), channel_id=1, source_target_pairs={{0,64},{64,128},{128,192},{1,65},{65,129},{129,193},{2,66},{66,130... | collective-permute-start | bytes 73736 | tf_op jit(solution)/shard_map/ppermute | solution.py:22
  147.6 7.6 %collective-permute-start.13 = (f32[1,48,128]{2,1,0:T(8,128)S(1)}, f32[1,48,128]{2,1,0:T(8,128)S(1)}, u32[]{:S(2)}, u32[]{:S(2)}) collective-permute-start(f32[1,48,128]{2,1,0:T(8,128)S(1)} %get-tuple-element.64), channel_id=1, source_target_pairs={{64,0},{128,64},{192,128},{65,1},{129,65},{193,129},{66,2},{130,66... | collective-permute-start | bytes 73736 | tf_op jit(solution)/shard_map/ppermute | solution.py:23
  148.9 12.7 %collective-permute-start.21 = (f32[10,1,64]{2,1,0:T(1,128)S(1)}, f32[10,1,64]{2,1,0:T(1,128)S(1)}, u32[]{:S(2)}, u32[]{:S(2)}) collective-permute-start(f32[10,1,64]{2,1,0:T(1,128)S(1)} %get-tuple-element.87), channel_id=1, source_target_pairs={{8,0},{16,8},{24,16},{32,24},{40,32},{48,40},{56,48},{9,1},{17,9},... | collective-permute-start | bytes 7688 | tf_op jit(solution)/shard_map/ppermute | solution.py:23
  150.2 11.4 %collective-permute-start.20 = (f32[10,1,64]{2,1,0:T(1,128)S(1)}, f32[10,1,64]{2,1,0:T(1,128)S(1)}, u32[]{:S(2)}, u32[]{:S(2)}) collective-permute-start(f32[10,1,64]{2,1,0:T(1,128)S(1)} %get-tuple-element.88), channel_id=1, source_target_pairs={{0,8},{8,16},{16,24},{24,32},{32,40},{40,48},{48,56},{1,9},{9,17},... | collective-permute-start | bytes 7688 | tf_op jit(solution)/shard_map/ppermute | solution.py:22
  166.5 14.4 %collective-permute-start.16 = (f32[18,50,1]{2,1,0:T(8,128)S(1)}, f32[18,50,1]{2,1,0:T(8,128)S(1)}, u32[]{:S(2)}, u32[]{:S(2)}) collective-permute-start(f32[18,50,1]{2,1,0:T(8,128)S(1)} %get-tuple-element.43), channel_id=1, source_target_pairs={{0,1},{1,2},{2,3},{3,4},{4,5},{5,6},{6,7},{8,9},{9,10},{10,11},{11... | collective-permute-start | bytes 10808 | tf_op jit(solution)/shard_map/ppermute | solution.py:22
  172.4 10.4 %collective-permute-start.17 = (f32[18,50,1]{2,1,0:T(8,128)S(1)}, f32[18,50,1]{2,1,0:T(8,128)S(1)}, u32[]{:S(2)}, u32[]{:S(2)}) collective-permute-start(f32[18,50,1]{2,1,0:T(8,128)S(1)} %get-tuple-element.44), channel_id=1, source_target_pairs={{1,0},{2,1},{3,2},{4,3},{5,4},{6,5},{7,6},{9,8},{10,9},{11,10},{12... | collective-permute-start | bytes 10808 | tf_op jit(solution)/shard_map/ppermute | solution.py:23
  175.1 45.7 %collective-permute-start.23 = (f32[10,26,1]{2,1,0:T(8,128)}, f32[10,26,1]{2,1,0:T(8,128)}, u32[]{:S(2)}, u32[]{:S(2)}) collective-permute-start(f32[10,26,1]{2,1,0:T(8,128)} %get-tuple-element.77), channel_id=1, source_target_pairs={{1,0},{2,1},{3,2},{4,3},{5,4},{6,5},{7,6},{9,8},{10,9},{11,10},{12... | collective-permute-start | bytes 3128 | tf_op jit(solution)/shard_map/ppermute | solution.py:23
  177.0 43.8 %collective-permute-start.22 = (f32[10,26,1]{2,1,0:T(8,128)}, f32[10,26,1]{2,1,0:T(8,128)}, u32[]{:S(2)}, u32[]{:S(2)}) collective-permute-start(f32[10,26,1]{2,1,0:T(8,128)} %get-tuple-element.78), channel_id=1, source_target_pairs={{0,1},{1,2},{2,3},{3,4},{4,5},{5,6},{6,7},{8,9},{9,10},{10,11},{11... | collective-permute-start | bytes 3128 | tf_op jit(solution)/shard_map/ppermute | solution.py:22
  231.4 12.0 %collective-permute-start.26 = (f32[10,1,64]{2,1,0:T(1,128)S(1)}, f32[10,1,64]{2,1,0:T(1,128)S(1)}, u32[]{:S(2)}, u32[]{:S(2)}) collective-permute-start(f32[10,1,64]{2,1,0:T(1,128)S(1)} %get-tuple-element.85), channel_id=1, source_target_pairs={{0,8},{8,16},{16,24},{24,32},{32,40},{40,48},{48,56},{1,9},{9,17},... | collective-permute-start | bytes 7688 | tf_op jit(solution)/shard_map/ppermute | solution.py:22
  236.2 7.2 %collective-permute-start.27 = (f32[10,1,64]{2,1,0:T(1,128)S(1)}, f32[10,1,64]{2,1,0:T(1,128)S(1)}, u32[]{:S(2)}, u32[]{:S(2)}) collective-permute-start(f32[10,1,64]{2,1,0:T(1,128)S(1)} %get-tuple-element.86), channel_id=1, source_target_pairs={{8,0},{16,8},{24,16},{32,24},{40,32},{48,40},{56,48},{9,1},{17,9},... | collective-permute-start | bytes 7688 | tf_op jit(solution)/shard_map/ppermute | solution.py:23
  238.1 30.2 %collective-permute-start.37 = (f32[1,12,32]{2,1,0:T(8,128)}, f32[1,12,32]{2,1,0:T(8,128)S(1)}, u32[]{:S(2)}, u32[]{:S(2)}) collective-permute-start(f32[1,12,32]{2,1,0:T(8,128)} %get-tuple-element.127), channel_id=1, source_target_pairs={{64,0},{128,64},{192,128},{65,1},{129,65},{193,129},{66,2},{130,66... | collective-permute-start | bytes 4616 | tf_op jit(solution)/shard_map/ppermute | solution.py:23
  239.4 28.9 %collective-permute-start.36 = (f32[1,12,32]{2,1,0:T(8,128)}, f32[1,12,32]{2,1,0:T(8,128)S(1)}, u32[]{:S(2)}, u32[]{:S(2)}) collective-permute-start(f32[1,12,32]{2,1,0:T(8,128)} %get-tuple-element.128), channel_id=1, source_target_pairs={{0,64},{64,128},{128,192},{1,65},{65,129},{129,193},{2,66},{66,130... | collective-permute-start | bytes 4616 | tf_op jit(solution)/shard_map/ppermute | solution.py:22
  244.3 18.0 %collective-permute-start.28 = (f32[10,26,1]{2,1,0:T(8,128)}, f32[10,26,1]{2,1,0:T(8,128)}, u32[]{:S(2)}, u32[]{:S(2)}) collective-permute-start(f32[10,26,1]{2,1,0:T(8,128)} %get-tuple-element.75), channel_id=1, source_target_pairs={{0,1},{1,2},{2,3},{3,4},{4,5},{5,6},{6,7},{8,9},{9,10},{10,11},{11... | collective-permute-start | bytes 3128 | tf_op jit(solution)/shard_map/ppermute | solution.py:22
  248.3 13.9 %collective-permute-start.29 = (f32[10,26,1]{2,1,0:T(8,128)}, f32[10,26,1]{2,1,0:T(8,128)}, u32[]{:S(2)}, u32[]{:S(2)}) collective-permute-start(f32[10,26,1]{2,1,0:T(8,128)} %get-tuple-element.76), channel_id=1, source_target_pairs={{1,0},{2,1},{3,2},{4,3},{5,4},{6,5},{7,6},{9,8},{10,9},{11,10},{12... | collective-permute-start | bytes 3128 | tf_op jit(solution)/shard_map/ppermute | solution.py:23
  264.1 10.5 %collective-permute-start.30 = (f32[1,24,64]{2,1,0:T(8,128)S(1)}, f32[1,24,64]{2,1,0:T(8,128)S(1)}, u32[]{:S(2)}, u32[]{:S(2)}) collective-permute-start(f32[1,24,64]{2,1,0:T(8,128)S(1)} %get-tuple-element.93), channel_id=1, source_target_pairs={{0,64},{64,128},{128,192},{1,65},{65,129},{129,193},{2,66},{66,130... | collective-permute-start | bytes 18440 | tf_op jit(solution)/shard_map/ppermute | solution.py:22
  267.0 7.6 %collective-permute-start.31 = (f32[1,24,64]{2,1,0:T(8,128)S(1)}, f32[1,24,64]{2,1,0:T(8,128)S(1)}, u32[]{:S(2)}, u32[]{:S(2)}) collective-permute-start(f32[1,24,64]{2,1,0:T(8,128)S(1)} %get-tuple-element.94), channel_id=1, source_target_pairs={{64,0},{128,64},{192,128},{65,1},{129,65},{193,129},{66,2},{130,66... | collective-permute-start | bytes 18440 | tf_op jit(solution)/shard_map/ppermute | solution.py:23
  268.4 11.2 %collective-permute-start.39 = (f32[6,1,32]{2,1,0:T(1,128)S(1)}, f32[6,1,32]{2,1,0:T(1,128)S(1)}, u32[]{:S(2)}, u32[]{:S(2)}) collective-permute-start(f32[6,1,32]{2,1,0:T(1,128)S(1)} %get-tuple-element.117), channel_id=1, source_target_pairs={{8,0},{16,8},{24,16},{32,24},{40,32},{48,40},{56,48},{9,1},{17,9},... | collective-permute-start | bytes 2312 | tf_op jit(solution)/shard_map/ppermute | solution.py:23
  269.7 9.9 %collective-permute-start.38 = (f32[6,1,32]{2,1,0:T(1,128)S(1)}, f32[6,1,32]{2,1,0:T(1,128)S(1)}, u32[]{:S(2)}, u32[]{:S(2)}) collective-permute-start(f32[6,1,32]{2,1,0:T(1,128)S(1)} %get-tuple-element.118), channel_id=1, source_target_pairs={{0,8},{8,16},{16,24},{24,32},{32,40},{40,48},{48,56},{1,9},{9,17},... | collective-permute-start | bytes 2312 | tf_op jit(solution)/shard_map/ppermute | solution.py:22
  282.8 13.8 %collective-permute-start.34 = (f32[10,26,1]{2,1,0:T(8,128)S(1)}, f32[10,26,1]{2,1,0:T(8,128)S(1)}, u32[]{:S(2)}, u32[]{:S(2)}) collective-permute-start(f32[10,26,1]{2,1,0:T(8,128)S(1)} %get-tuple-element.73), channel_id=1, source_target_pairs={{0,1},{1,2},{2,3},{3,4},{4,5},{5,6},{6,7},{8,9},{9,10},{10,11},{11... | collective-permute-start | bytes 3128 | tf_op jit(solution)/shard_map/ppermute | solution.py:22
  288.4 8.2 %collective-permute-start.35 = (f32[10,26,1]{2,1,0:T(8,128)S(1)}, f32[10,26,1]{2,1,0:T(8,128)S(1)}, u32[]{:S(2)}, u32[]{:S(2)}) collective-permute-start(f32[10,26,1]{2,1,0:T(8,128)S(1)} %get-tuple-element.74), channel_id=1, source_target_pairs={{1,0},{2,1},{3,2},{4,3},{5,4},{6,5},{7,6},{9,8},{10,9},{11,10},{12... | collective-permute-start | bytes 3128 | tf_op jit(solution)/shard_map/ppermute | solution.py:23
  291.1 14.7 %collective-permute-start.41 = (f32[6,14,1]{2,1,0:T(8,128)}, f32[6,14,1]{2,1,0:T(8,128)}, u32[]{:S(2)}, u32[]{:S(2)}) collective-permute-start(f32[6,14,1]{2,1,0:T(8,128)} %get-tuple-element.115), channel_id=1, source_target_pairs={{1,0},{2,1},{3,2},{4,3},{5,4},{6,5},{7,6},{9,8},{10,9},{11,10},{12... | collective-permute-start | bytes 1016 | tf_op jit(solution)/shard_map/ppermute | solution.py:23
  293.0 12.8 %collective-permute-start.40 = (f32[6,14,1]{2,1,0:T(8,128)}, f32[6,14,1]{2,1,0:T(8,128)}, u32[]{:S(2)}, u32[]{:S(2)}) collective-permute-start(f32[6,14,1]{2,1,0:T(8,128)} %get-tuple-element.116), channel_id=1, source_target_pairs={{0,1},{1,2},{2,3},{3,4},{4,5},{5,6},{6,7},{8,9},{9,10},{10,11},{11... | collective-permute-start | bytes 1016 | tf_op jit(solution)/shard_map/ppermute | solution.py:22
  316.1 9.3 %collective-permute-start.44 = (f32[6,1,32]{2,1,0:T(1,128)S(1)}, f32[6,1,32]{2,1,0:T(1,128)S(1)}, u32[]{:S(2)}, u32[]{:S(2)}) collective-permute-start(f32[6,1,32]{2,1,0:T(1,128)S(1)} %get-tuple-element.113), channel_id=1, source_target_pairs={{0,8},{8,16},{16,24},{24,32},{32,40},{40,48},{48,56},{1,9},{9,17},... | collective-permute-start | bytes 2312 | tf_op jit(solution)/shard_map/ppermute | solution.py:22
  322.0 21.1 %collective-permute-start.54 = (f32[1,6,16]{2,0,1:T(1,128)}, f32[1,6,16]{2,0,1:T(1,128)S(1)}, u32[]{:S(2)}, u32[]{:S(2)}) collective-permute-start(f32[1,6,16]{2,0,1:T(1,128)} %get-tuple-element.163), channel_id=1, source_target_pairs={{0,64},{64,128},{128,192},{1,65},{65,129},{129,193},{2,66},{66,130... | collective-permute-start | bytes 1160 | tf_op jit(solution)/shard_map/ppermute | solution.py:22
  324.1 19.1 %collective-permute-start.55 = (f32[1,6,16]{2,0,1:T(1,128)}, f32[1,6,16]{2,0,1:T(1,128)}, u32[]{:S(2)}, u32[]{:S(2)}) collective-permute-start(f32[1,6,16]{2,0,1:T(1,128)} %get-tuple-element.164), channel_id=1, source_target_pairs={{64,0},{128,64},{192,128},{65,1},{129,65},{193,129},{66,2},{130,66... | collective-permute-start | bytes 1160 | tf_op jit(solution)/shard_map/ppermute | solution.py:23
  326.2 10.3 %collective-permute-start.46 = (f32[6,14,1]{2,1,0:T(8,128)}, f32[6,14,1]{2,1,0:T(8,128)}, u32[]{:S(2)}, u32[]{:S(2)}) collective-permute-start(f32[6,14,1]{2,1,0:T(8,128)} %get-tuple-element.111), channel_id=1, source_target_pairs={{0,1},{1,2},{2,3},{3,4},{4,5},{5,6},{6,7},{8,9},{9,10},{10,11},{11... | collective-permute-start | bytes 1016 | tf_op jit(solution)/shard_map/ppermute | solution.py:22
  337.9 12.2 %collective-permute-start.48 = (f32[1,12,32]{2,1,0:T(8,128)S(1)}, f32[1,12,32]{2,1,0:T(8,128)S(1)}, u32[]{:S(2)}, u32[]{:S(2)}) collective-permute-start(f32[1,12,32]{2,1,0:T(8,128)S(1)} %get-tuple-element.123), channel_id=1, source_target_pairs={{0,64},{64,128},{128,192},{1,65},{65,129},{129,193},{2,66},{66,130... | collective-permute-start | bytes 4616 | tf_op jit(solution)/shard_map/ppermute | solution.py:22
  341.8 8.2 %collective-permute-start.49 = (f32[1,12,32]{2,1,0:T(8,128)S(1)}, f32[1,12,32]{2,1,0:T(8,128)S(1)}, u32[]{:S(2)}, u32[]{:S(2)}) collective-permute-start(f32[1,12,32]{2,1,0:T(8,128)S(1)} %get-tuple-element.124), channel_id=1, source_target_pairs={{64,0},{128,64},{192,128},{65,1},{129,65},{193,129},{66,2},{130,66... | collective-permute-start | bytes 4616 | tf_op jit(solution)/shard_map/ppermute | solution.py:23
  343.8 11.2 %collective-permute-start.57 = (f32[4,1,16]{2,0,1:T(4,128)S(1)}, f32[4,1,16]{2,0,1:T(4,128)S(1)}, u32[]{:S(2)}, u32[]{:S(2)}) collective-permute-start(f32[4,1,16]{2,0,1:T(4,128)S(1)} %get-tuple-element.151), channel_id=1, source_target_pairs={{8,0},{16,8},{24,16},{32,24},{40,32},{48,40},{56,48},{9,1},{17,9},... | collective-permute-start | bytes 776 | tf_op jit(solution)/shard_map/ppermute | solution.py:23
  345.1 9.9 %collective-permute-start.56 = (f32[4,1,16]{2,0,1:T(4,128)S(1)}, f32[4,1,16]{2,0,1:T(4,128)S(1)}, u32[]{:S(2)}, u32[]{:S(2)}) collective-permute-start(f32[4,1,16]{2,0,1:T(4,128)S(1)} %get-tuple-element.152), channel_id=1, source_target_pairs={{0,8},{8,16},{16,24},{24,32},{32,40},{40,48},{48,56},{1,9},{9,17},... | collective-permute-start | bytes 776 | tf_op jit(solution)/shard_map/ppermute | solution.py:22
  358.2 13.8 %collective-permute-start.52 = (f32[6,14,1]{2,1,0:T(8,128)S(1)}, f32[6,14,1]{2,1,0:T(8,128)S(1)}, u32[]{:S(2)}, u32[]{:S(2)}) collective-permute-start(f32[6,14,1]{2,1,0:T(8,128)S(1)} %get-tuple-element.107), channel_id=1, source_target_pairs={{0,1},{1,2},{2,3},{3,4},{4,5},{5,6},{6,7},{8,9},{9,10},{10,11},{11... | collective-permute-start | bytes 1016 | tf_op jit(solution)/shard_map/ppermute | solution.py:22
  363.8 8.2 %collective-permute-start.53 = (f32[6,14,1]{2,1,0:T(8,128)S(1)}, f32[6,14,1]{2,1,0:T(8,128)S(1)}, u32[]{:S(2)}, u32[]{:S(2)}) collective-permute-start(f32[6,14,1]{2,1,0:T(8,128)S(1)} %get-tuple-element.108), channel_id=1, source_target_pairs={{1,0},{2,1},{3,2},{4,3},{5,4},{6,5},{7,6},{9,8},{10,9},{11,10},{12... | collective-permute-start | bytes 1016 | tf_op jit(solution)/shard_map/ppermute | solution.py:23
  366.4 10.6 %collective-permute-start.59 = (f32[4,8,1]{2,0,1:T(4,128)}, f32[4,8,1]{2,0,1:T(4,128)}, u32[]{:S(2)}, u32[]{:S(2)}) collective-permute-start(f32[4,8,1]{2,0,1:T(4,128)} %get-tuple-element.139), channel_id=1, source_target_pairs={{1,0},{2,1},{3,2},{4,3},{5,4},{6,5},{7,6},{9,8},{10,9},{11,10},{12... | collective-permute-start | bytes 392 | tf_op jit(solution)/shard_map/ppermute | solution.py:23
  368.3 8.7 %collective-permute-start.58 = (f32[4,8,1]{2,0,1:T(4,128)}, f32[4,8,1]{2,0,1:T(4,128)}, u32[]{:S(2)}, u32[]{:S(2)}) collective-permute-start(f32[4,8,1]{2,0,1:T(4,128)} %get-tuple-element.140), channel_id=1, source_target_pairs={{0,1},{1,2},{2,3},{3,4},{4,5},{5,6},{6,7},{8,9},{9,10},{10,11},{11... | collective-permute-start | bytes 392 | tf_op jit(solution)/shard_map/ppermute | solution.py:22
  395.8 6.9 %collective-permute-start.64 = (f32[4,8,1]{2,0,1:T(4,128)S(1)}, f32[4,8,1]{2,0,1:T(4,128)S(1)}, u32[]{:S(2)}, u32[]{:S(2)}) collective-permute-start(f32[4,8,1]{2,0,1:T(4,128)S(1)} %get-tuple-element.137), channel_id=1, source_target_pairs={{0,1},{1,2},{2,3},{3,4},{4,5},{5,6},{6,7},{8,9},{9,10},{10,11},{11... | collective-permute-start | bytes 392 | tf_op jit(solution)/shard_map/ppermute | solution.py:22
  602.7 6.9 %collective-permute-start.112 = (f32[10,26,1]{2,1,0:T(8,128)S(1)}, f32[10,26,1]{2,1,0:T(8,128)S(1)}, u32[]{:S(2)}, u32[]{:S(2)}) collective-permute-start(f32[10,26,1]{2,1,0:T(8,128)S(1)} %get-tuple-element.69), channel_id=1, source_target_pairs={{0,1},{1,2},{2,3},{3,4},{4,5},{5,6},{6,7},{8,9},{9,10},{10,11},{11... | collective-permute-start | bytes 3128 | tf_op jit(solution)/shard_map/ppermute | solution.py:22
  634.0 10.6 %collective-permute-start.118 = (f32[18,50,1]{2,1,0:T(8,128)S(1)}, f32[18,50,1]{2,1,0:T(8,128)S(1)}, u32[]{:S(2)}, u32[]{:S(2)}) collective-permute-start(f32[18,50,1]{2,1,0:T(8,128)S(1)} %get-tuple-element.41), channel_id=1, source_target_pairs={{0,1},{1,2},{2,3},{3,4},{4,5},{5,6},{6,7},{8,9},{9,10},{10,11},{11... | collective-permute-start | bytes 10808 | tf_op jit(solution)/shard_map/ppermute | solution.py:22
  638.6 10.4 %collective-permute-start.119 = (f32[18,50,1]{2,1,0:T(8,128)S(1)}, f32[18,50,1]{2,1,0:T(8,128)S(1)}, u32[]{:S(2)}, u32[]{:S(2)}) collective-permute-start(f32[18,50,1]{2,1,0:T(8,128)S(1)} %get-tuple-element.42), channel_id=1, source_target_pairs={{1,0},{2,1},{3,2},{4,3},{5,4},{6,5},{7,6},{9,8},{10,9},{11,10},{12... | collective-permute-start | bytes 10808 | tf_op jit(solution)/shard_map/ppermute | solution.py:23
  664.5 10.4 %collective-permute-start.124 = (f32[18,50,1]{2,1,0:T(8,128)S(1)}, f32[18,50,1]{2,1,0:T(8,128)S(1)}, u32[]{:S(2)}, u32[]{:S(2)}) collective-permute-start(f32[18,50,1]{2,1,0:T(8,128)S(1)} %get-tuple-element.39), channel_id=1, source_target_pairs={{0,1},{1,2},{2,3},{3,4},{4,5},{5,6},{6,7},{8,9},{9,10},{10,11},{11... | collective-permute-start | bytes 10808 | tf_op jit(solution)/shard_map/ppermute | solution.py:22
  668.9 10.4 %collective-permute-start.125 = (f32[18,50,1]{2,1,0:T(8,128)S(1)}, f32[18,50,1]{2,1,0:T(8,128)S(1)}, u32[]{:S(2)}, u32[]{:S(2)}) collective-permute-start(f32[18,50,1]{2,1,0:T(8,128)S(1)} %get-tuple-element.40), channel_id=1, source_target_pairs={{1,0},{2,1},{3,2},{4,3},{5,4},{6,5},{7,6},{9,8},{10,9},{11,10},{12... | collective-permute-start | bytes 10808 | tf_op jit(solution)/shard_map/ppermute | solution.py:23
  (105 other events, 1487.0 us)
where the time goes:
time: 687 us; the launch traced here: 682 us
  starting transfers between devices  331 us (48%)
  waiting for transfers between devices  147 us (21%)
  local copies, waits for them, and re-layouts  127 us (18%)
  other arithmetic  74.5 us (11%)
    ppermute x63, starting transfers between devices, padded_2(): before = lax.ppermute(last, axis, up)  233 us
    ppermute x63, waiting for transfers between devices, padded_2(): after = lax.ppermute(initial, axis, down)  136 us
    ppermute x63, starting transfers between devices, padded_2(): after = lax.ppermute(initial, axis, down)  97.9 us
    reshape x5, local copies, waits for them, and re-layouts, coarsen(): values.reshape(shape[0] // 2, 2, shape[1] // 2, 2, shape[2] // 2, 2)  87.7 us
    reduce_sum x9, other arithmetic, coarsen(): values.reshape(shape[0] // 2, 2, shape[1] // 2, 2, shape[2] // 2, 2)  40 us
    add x11, other arithmetic, smooth(): approx = approx + update  14.9 us
    div x6, local copies, waits for them, and re-layouts, coarsen(): values.reshape(shape[0] // 2, 2, shape[1] // 2, 2, shape[2] // 2, 2)  14.8 us
  transfers between devices with their start and end apart: 126, of which 48 were waited for; matrix products, arithmetic and copies ran while one was open for 24% of the time, Pallas kernels for 0%

commit v1 on v0

v1 whole, which is shorter than its diff:
```python
import jax
import jax.numpy as jnp
from jax import lax
from jax.experimental import pallas as pl
from jax.experimental.pallas import tpu as pltpu
from jax.sharding import PartitionSpec as P

LEVELS = 4
COARSE_SWEEPS = 6
CENTRE = 1.1
RADIUS = 0.9
LANES = 128
PAD = 8

MESH = pl.DeviceIdType.MESH
AXES = ("gx", "gy", "gz")


def chebyshev(sweeps):
    ratio = RADIUS / CENTRE
    factors = [(0.0, 1.0 / CENTRE)]
    for _ in range(sweeps - 1):
        following = 1.0 / (2.0 * CENTRE / RADIUS - ratio)
        factors.append((following * ratio, 2.0 * following / RADIUS))
        ratio = following
    return factors


def round_up(value):
    return -(-value // 8) * 8


class Names:
    pass


def exact_dot(left, matrix):
    high = left.astype(jnp.bfloat16)
    rest = left - high.astype(jnp.float32)
    middle = rest.astype(jnp.bfloat16)
    low = (rest - middle.astype(jnp.float32)).astype(jnp.bfloat16)
    total = jnp.dot(low, matrix, preferred_element_type=jnp.float32)
    total = total + jnp.dot(middle, matrix, preferred_element_type=jnp.float32)
    return total + jnp.dot(high, matrix, preferred_element_type=jnp.float32)


def make_kernel(shape, sizes, plan):
    count = {axis: sizes[axis] for axis in AXES}

    def kernel(rhs, coef_b, coef_c, out, *scratch):
        refs = plan.unpack(scratch)
        place = {axis: lax.axis_index(axis) for axis in AXES}
        after = {axis: lax.rem(place[axis] + 1, count[axis]) for axis in AXES}
        before = {axis: lax.rem(place[axis] + count[axis] - 1, count[axis]) for axis in AXES}
        has_before = {a: jnp.where(place[a] > 0, 1.0, 0.0).astype(jnp.float32) for a in AXES}
        has_after = {a: jnp.where(place[a] < count[a] - 1, 1.0, 0.0).astype(jnp.float32) for a in AXES}

        barrier = pltpu.get_barrier_semaphore()
        for axis in AXES:
            for other in (before[axis], after[axis]):
                pl.semaphore_signal(barrier, inc=1, device_id={axis: other}, device_id_type=MESH)
        pl.semaphore_wait(barrier, 6)

        lane = lax.broadcasted_iota(jnp.int32, (1, LANES), 1)

        def dims(level):
            return tuple(n >> level for n in shape)

        def copies(level, h):
            nx, ny, _ = dims(level)
            rows = pl.ds(PAD, round_up(ny))
            vp, zs, zr, ys, yr = h.vp, h.zs, h.zr, h.ys, h.yr
            pairs = (
                (vp.at[nx, rows], vp.at[0, rows], "gx", after),
                (vp.at[1, rows], vp.at[nx + 1, rows], "gx", before),
                (ys.at[0], yr.at[0], "gy", after),
                (ys.at[1], yr.at[1], "gy", before),
                (zs.at[0], zr.at[0], "gz", after),
                (zs.at[1], zr.at[1], "gz", before),
            )
            return [
                pltpu.make_async_remote_copy(
                    src_ref=src, dst_ref=dst, send_sem=h.send.at[i], recv_sem=h.recv.at[i],
                    device_id={axis: where[axis]}, device_id_type=MESH)
                for i, (src, dst, axis, where) in enumerate(pairs)
            ]

        def start(level, h):
            for copy in copies(level, h):
                copy.start()

        def finish(level, h):
            nx, ny, _ = dims(level)
            for copy in copies(level, h):
                copy.wait()
            for x in range(nx):
                h.vp[x + 1, pl.ds(PAD - 1, 1), :] = h.yr[0, pl.ds(x, 1), :]
                h.vp[x + 1, pl.ds(PAD + ny, 1), :] = h.yr[1, pl.ds(x, 1), :]

        def sweep(level, make, h=None, extra=()):
            nx, ny, nz = dims(level)
            zero = jnp.zeros((ny, LANES), jnp.float32)

            def body(x, carry):
                high, low = carry
                plane = make(x)
                h.vp[x + 1, pl.ds(PAD, ny), :] = plane
                h.ys[0, pl.ds(x, 1), :] = plane[ny - 1:ny]
                h.ys[1, pl.ds(x, 1), :] = plane[0:1]
                here = lane == x
                high = jnp.where(here, pltpu.roll(plane, lax.rem(x + LANES - (nz - 1), LANES), 1), high)
                low = jnp.where(here, pltpu.roll(plane, x, 1), low)
                return high, low

            high, low = lax.fori_loop(0, nx, body, (zero, zero))
            h.zs[0, pl.ds(0, ny), :] = high
            h.zs[1, pl.ds(0, ny), :] = low
            start(level, h)

        def around(level, h, x):
            nx, ny, nz = dims(level)
            vp = h.vp
            mid = vp[x + 1, pl.ds(PAD, ny), :]
            zlow = h.zr[0, pl.ds(0, ny), :]
            zhigh = h.zr[1, pl.ds(0, ny), :]
            zm = jnp.where(lane == 0, pltpu.roll(zlow, lax.rem(LANES - x, LANES), 1), pltpu.roll(mid, 1, 1))
            zp = jnp.where(lane == nz - 1, pltpu.roll(zhigh, lax.rem(LANES + nz - 1 - x, LANES), 1),
                           pltpu.roll(mid, LANES - 1, 1))
            return (mid, vp[x, pl.ds(PAD, ny), :], vp[x + 2, pl.ds(PAD, ny), :],
                    vp[x + 1, pl.ds(PAD - 1, ny), :], vp[x + 1, pl.ds(PAD + 1, ny), :], zm, zp)

        def residual(level, h, x):
            g = refs.level[level]
            mid, xm, xp, ym, yp, zm, zp = around(level, h, x)
            total = g.sx[x] * xm + g.sx[x + 1] * xp + g.sym[x] * ym + g.syp[x] * yp + g.szm[x] * zm + g.szp[x] * zp
            return mid, source(level, x) - g.q[x] * mid + total

        def source(level, x):
            return rhs[x] if level == 0 else refs.level[level].f[x]

        def reaction(level, x):
            return coef_c[x] if level == 0 else refs.level[level].c[x]

        row_of = lax.broadcasted_iota(jnp.int32, (LANES, LANES), 0)
        col_of = lax.broadcasted_iota(jnp.int32, (LANES, LANES), 1)
        shrink = jnp.where((row_of // 2 == col_of), 0.125, 0.0).astype(jnp.bfloat16)
        grow = jnp.where((col_of // 2 == row_of), 1.0, 0.0).astype(jnp.bfloat16)

        def coarsen(level, get, put):
            nx, ny, nz = dims(level)
            pair = refs.level[level].pair

            def body(x, carry):
                pair[x] = get(2 * x) + get(2 * x + 1)
                return carry

            lax.fori_loop(0, nx // 2, body, 0)
            for x in range(nx // 2):
                even = pair[x, pl.ds(0, ny // 2, 2), :]
                odd = pair[x, pl.ds(1, ny // 2, 2), :]
                mean = exact_dot(even + odd, shrink)
                put(x, jnp.where(lane < nz // 2, mean, 0.0))

        def refine(level, get):
            nx, ny, nz = dims(level)
            pair = refs.level[level].pair
            for x in range(nx // 2):
                wide = exact_dot(get(x), grow)
                pair[x, pl.ds(0, ny // 2, 2), :] = wide
                pair[x, pl.ds(1, ny // 2, 2), :] = wide

        for level in range(LEVELS):
            ny = dims(level)[1]
            if level == 0:
                sweep(level, lambda x: coef_b[x], refs.level[level].b)
            else:
                g = refs.level[level]
                upper = refs.level[level - 1]
                above_y = dims(level - 1)[1]

                def put_b(x, plane, g=g, ny=ny):
                    g.f[x] = plane

                def put_c(x, plane, g=g):
                    g.c[x] = plane

                coarsen(level - 1, lambda x: upper.b.vp[x + 1, pl.ds(PAD, above_y), :], put_b)
                coarsen(level - 1, lambda x: reaction(level - 1, x), put_c)
                sweep(level, lambda x: g.f[x], g.b)

        def setup(level):
            g = refs.level[level]
            nx, ny, nz = dims(level)
            half = 0.5 * 4.0 ** (LEVELS - 1 - level)
            finish(level, g.b)
            g.b.vp[0, pl.ds(PAD, ny), :] = g.b.vp[0, pl.ds(PAD, ny), :] * has_before["gx"]
            g.b.vp[nx + 1, pl.ds(PAD, ny), :] = g.b.vp[nx + 1, pl.ds(PAD, ny), :] * has_after["gx"]
            row = lax.broadcasted_iota(jnp.int32, (ny, 1), 0)
            keep_ym = jnp.where(row == 0, has_before["gy"], 1.0)
            keep_yp = jnp.where(row == ny - 1, has_after["gy"], 1.0)
            keep_zm = jnp.where(lane == 0, has_before["gz"], 1.0)
            keep_zp = jnp.where(lane == nz - 1, has_after["gz"], 1.0)

            def body(x, carry):
                mid, xm, xp, ym, yp, zm, zp = around(level, g.b, x)
                fxm, fxp = half * (mid + xm), half * (mid + xp)
                fym, fyp = half * (mid + ym * keep_ym), half * (mid + yp * keep_yp)
                fzm, fzp = half * (mid + zm * keep_zm), half * (mid + zp * keep_zp)
                q = reaction(level, x) + (fxm + fxp + fym + fyp + fzm + fzp)
                g.q[x] = q
                g.rq[x] = jnp.where(lane < nz, 1.0 / q, 0.0)
                g.sx[x] = fxm * jnp.where(x == 0, has_before["gx"], 1.0)
                g.sym[x] = fym * keep_ym
                g.syp[x] = fyp * keep_yp
                g.szm[x] = fzm * keep_zm
                g.szp[x] = fzp * keep_zp
                return carry

            lax.fori_loop(0, nx, body, 0)
            last = g.b.vp[nx, pl.ds(PAD, ny), :] + g.b.vp[nx + 1, pl.ds(PAD, ny), :]
            g.sx[nx] = half * last * has_after["gx"]

        steps = chebyshev(2)
        (_, first), (carry_e, weight_r) = steps

        for level in range(LEVELS - 1):
            g = refs.level[level]
            setup(level)
            sweep(level, lambda x: source(level, x) * g.rq[x] * first, g.it[0])
            finish(level, g.it[0])

            def second(x):
                mid, rest = residual(level, g.it[0], x)
                return mid * (1.0 + carry_e) + weight_r * rest * g.rq[x]

            sweep(level, second, g.it[1])
            finish(level, g.it[1])
            below = refs.level[level + 1]

            def put_f(x, plane, below=below):
                below.f[x] = plane

            coarsen(level, lambda x: residual(level, g.it[1], x)[1], put_f)

        level = LEVELS - 1
        g = refs.level[level]
        setup(level)
        steps = chebyshev(COARSE_SWEEPS)

        def begin(x):
            update = source(level, x) * g.rq[x] * steps[0][1]
            g.e[x] = update
            return update

        sweep(level, begin, g.it[0])
        for step in range(1, COARSE_SWEEPS):
            finish(level, g.it[step - 1])

            def advance(x, step=step):
                mid, rest = residual(level, g.it[step - 1], x)
                update = steps[step][0] * g.e[x] + steps[step][1] * rest * g.rq[x]
                g.e[x] = update
                return mid + update

            if step < COARSE_SWEEPS - 1:
                sweep(level, advance, g.it[step])
            else:
                for x in range(dims(level)[0]):
                    g.f[x] = advance(x)

        for level in range(LEVELS - 2, -1, -1):
            g = refs.level[level]
            nx, ny, nz = dims(level)
            below = refs.level[level + 1]
            refine(level, lambda x: below.f[x])
            sweep(level, lambda x: g.it[1].vp[x + 1, pl.ds(PAD, ny), :] + g.pair[x // 2], g.it[2])
            finish(level, g.it[2])

            def third(x):
                mid, rest = residual(level, g.it[2], x)
                update = first * rest * g.rq[x]
                g.e[x] = update
                return mid + update

            sweep(level, third, g.it[3])
            finish(level, g.it[3])

            def last(x, carry):
                mid, rest = residual(level, g.it[3], x)
                result = mid + carry_e * g.e[x] + weight_r * rest * g.rq[x]
                if level == 0:
                    out[x] = result
                else:
                    g.f[x] = result
                return carry

            lax.fori_loop(0, nx, last, 0)

    return kernel


class Plan:
    def __init__(self, shape):
        self.shapes = []
        self.tree = Names()
        self.tree.level = []
        for level in range(LEVELS):
            nx, ny, _ = (n >> level for n in shape)
            g = Names()

            def planes(n, ny=ny):
                return self.add(pltpu.VMEM((n, ny, LANES), jnp.float32))

            def halo(nx=nx, ny=ny):
                h = Names()
                h.vp = self.add(pltpu.VMEM((nx + 2, round_up(ny) + 2 * PAD, LANES), jnp.float32))
                h.zs = self.add(pltpu.VMEM((2, round_up(ny), LANES), jnp.float32))
                h.zr = self.add(pltpu.VMEM((2, round_up(ny), LANES), jnp.float32))
                h.ys = self.add(pltpu.VMEM((2, round_up(nx), LANES), jnp.float32))
                h.yr = self.add(pltpu.VMEM((2, round_up(nx), LANES), jnp.float32))
                h.send = self.add(pltpu.SemaphoreType.DMA((6,)))
                h.recv = self.add(pltpu.SemaphoreType.DMA((6,)))
                return h

            g.b = halo()
            g.sx = planes(nx + 1)
            for name in ("sym", "syp", "szm", "szp", "q", "rq", "e"):
                setattr(g, name, planes(nx))
            if level > 0:
                g.f = planes(nx)
                g.c = planes(nx)
            if level < LEVELS - 1:
                g.pair = planes(nx // 2)
            g.it = [halo() for _ in range(COARSE_SWEEPS - 1 if level == LEVELS - 1 else 4)]
            self.tree.level.append(g)

    def add(self, shape):
        self.shapes.append(shape)
        return len(self.shapes) - 1

    def unpack(self, refs):
        def walk(node):
            if isinstance(node, int):
                return refs[node]
            if isinstance(node, list):
                return [walk(item) for item in node]
            result = Names()
            for name, item in vars(node).items():
                setattr(result, name, walk(item))
            return result

        return walk(self.tree)


def solution(mesh):
    sizes = dict(mesh.shape)

    def local(rhs, coef_b, coef_c):
        shape = rhs.shape
        plan = Plan(shape)
        return pl.pallas_call(
            make_kernel(shape, sizes, plan),
            out_shape=jax.ShapeDtypeStruct(shape, jnp.float32),
            in_specs=[pl.BlockSpec(memory_space=pltpu.VMEM)] * 3,
            out_specs=pl.BlockSpec(memory_space=pltpu.VMEM),
            scratch_shapes=plan.shapes,
            compiler_params=pltpu.CompilerParams(
                collective_id=0, has_side_effects=True, vmem_limit_bytes=40 * 2**20),
        )(rhs, coef_b, coef_c)

    return jax.shard_map(
        local,
        mesh=mesh,
        in_specs=(P(*AXES),) * 3,
        out_specs=P(*AXES),
        check_vma=False,
    )
```

time: 687 us -> 99.7 us (0.15)
  starting transfers between devices: 331 us -> 0 us
  waiting for transfers between devices: 147 us -> 0 us
  local copies, waits for them, and re-layouts: 127 us -> 3.73 us
  Pallas kernels: 0 us -> 95.8 us
  other arithmetic: 74.5 us -> 0 us
    ppermute x126 -> x0, starting transfers between devices: 331 us -> none  [the longest x63 233 us: padded_2(): before = lax.ppermute(last, axis, up)]
    ppermute x126 -> x0, waiting for transfers between devices: 147 us -> none  [the longest x63 136 us: padded_2(): after = lax.ppermute(initial, axis, down)]
    pallas_call x0 -> x1, Pallas kernels: none -> 95.8 us  [local(): pl.pallas_call(make_kernel(shape, sizes, plan), out_shape=jax.ShapeDtypeS...]
    reshape x11 -> x0, local copies, waits for them, and re-layouts: 95.2 us -> none  [the longest x5 87.7 us: coarsen(): values.reshape(shape[0] // 2, 2, shape[1] // 2, 2, shape[2] // 2, 2)]
    reduce_sum x9 -> x0, other arithmetic: 40 us -> none  [coarsen(): values.reshape(shape[0] // 2, 2, shape[1] // 2, 2, shape[2] // 2, 2)]
    add x17 -> x0, other arithmetic: 20.3 us -> none  [the longest x11 14.9 us: smooth(): approx = approx + update]
    div x6 -> x0, local copies, waits for them, and re-layouts: 14.8 us -> none  [coarsen(): values.reshape(shape[0] // 2, 2, shape[1] // 2, 2, shape[2] // 2, 2)]
    slice x43 -> x0, local copies, waits for them, and re-layouts: 9.14 us -> none  [the longest x35 4.8 us: padded_2(): last = lax.slice_in_dim(value, length - width, length, axis=dim)]
  transfers between devices with their start and end apart: 126 -> 0, of which waited for: 48 -> 0; matrix products, arithmetic and copies ran while one was open for 24% -> 0% of each run, Pallas kernels for 0% -> 0%
where the time goes in v1:
time: 99.7 us; the launch traced here: 99.5 us
  Pallas kernels  95.8 us (96%)
  local copies, waits for them, and re-layouts  3.73 us (4%)
    pallas_call x1, Pallas kernels, local(): pl.pallas_call(make_kernel(shape, sizes, plan), out_shape=jax.ShapeDtypeS...  95.8 us
    unnamed x7, local copies, waits for them, and re-layouts  3.73 us

profile of v1, /device:TPU:1, one launch (start us, length us, event | category | flops | bytes accessed | tf_op | source)
XLA Modules:
  0.0 99.5 jit_solution(15170796230464422992)
XLA Ops:
  0.0 0.0 copy-start
  0.0 1.0 copy-done
  1.0 0.0 copy-start.1
  1.0 1.0 copy-done.1
  2.0 0.0 copy-start.2
  2.0 1.0 copy-done.2
  3.0 95.8 %shard_map.37 = f32[16,48,128]{2,1,0:T(8,128)S(1)} custom-call(f32[16,48,128]{2,1,0:T(8,128)S(1)} %copy-done, f32[16,48,128]{2,1,0:T(8,128)S(1)} %copy-done.1, f32[16,48,128]{2,1,0:T(8,128)S(1)} %copy-done.2), custom_call_target="tpu_custom_call" | custom-call | tf_op jit(solution)/shard_map/pallas_call | solution.py:361
  98.8 0.7 copy.5
Async XLA Ops:
  0.0 1.0 %copy-start = (f32[16,48,128]{2,1,0:T(8,128)S(1)}, f32[16,48,128]{2,1,0:T(8,128)}, u32[]{:S(2)}) copy-start(f32[16,48,128]{2,1,0:T(8,128)} %rhs.1) | copy-start | bytes 1179652
  1.0 1.0 %copy-start.1 = (f32[16,48,128]{2,1,0:T(8,128)S(1)}, f32[16,48,128]{2,1,0:T(8,128)}, u32[]{:S(2)}) copy-start(f32[16,48,128]{2,1,0:T(8,128)} %coef_b.1) | copy-start | bytes 1179652
  2.0 1.0 %copy-start.2 = (f32[16,48,128]{2,1,0:T(8,128)S(1)}, f32[16,48,128]{2,1,0:T(8,128)}, u32[]{:S(2)}) copy-start(f32[16,48,128]{2,1,0:T(8,128)} %coef_c.1) | copy-start | bytes 1179652

commit v2 on v1

v2 whole, which is shorter than its diff:
```python
import jax
import jax.numpy as jnp
from jax import lax
from jax.experimental import pallas as pl
from jax.experimental.pallas import tpu as pltpu
from jax.sharding import PartitionSpec as P

LEVELS = 4
COARSE_SWEEPS = 6
CENTRE = 1.1
RADIUS = 0.9
LANES = 128
PAD = 8

MESH = pl.DeviceIdType.MESH
AXES = ("gx", "gy", "gz")


def chebyshev(sweeps):
    ratio = RADIUS / CENTRE
    factors = [(0.0, 1.0 / CENTRE)]
    for _ in range(sweeps - 1):
        following = 1.0 / (2.0 * CENTRE / RADIUS - ratio)
        factors.append((following * ratio, 2.0 * following / RADIUS))
        ratio = following
    return factors


def round_up(value):
    return -(-value // 8) * 8


class Names:
    pass


def exact_dot(left, matrix):
    high = left.astype(jnp.bfloat16)
    rest = left - high.astype(jnp.float32)
    middle = rest.astype(jnp.bfloat16)
    low = (rest - middle.astype(jnp.float32)).astype(jnp.bfloat16)
    total = jnp.dot(low, matrix, preferred_element_type=jnp.float32)
    total = total + jnp.dot(middle, matrix, preferred_element_type=jnp.float32)
    return total + jnp.dot(high, matrix, preferred_element_type=jnp.float32)


WINDOW = (None, None, (16, 48), (8, 24))
FIRST_ROW = (0, 0, 18, 9)
NEAR = (-2, -1, 1, 2)


def make_kernel(shape, sizes, plan):
    count = {axis: sizes[axis] for axis in AXES}

    def kernel(rhs, coef_b, coef_c, out, *scratch):
        refs = plan.unpack(scratch)
        place = {axis: lax.axis_index(axis) for axis in AXES}

        def beyond(axis, step):
            return lax.rem(place[axis] + count[axis] + step, count[axis])

        after = {axis: beyond(axis, 1) for axis in AXES}
        before = {axis: beyond(axis, -1) for axis in AXES}
        has_before = {a: jnp.where(place[a] > 0, 1.0, 0.0).astype(jnp.float32) for a in AXES}
        has_after = {a: jnp.where(place[a] < count[a] - 1, 1.0, 0.0).astype(jnp.float32) for a in AXES}
        around_xz = [(dx, dz) for dx in range(4) for dz in (-1, 0, 1) if (dx, dz) != (0, 0)]

        barrier = pltpu.get_barrier_semaphore()
        for dy in NEAR:
            pl.semaphore_signal(barrier, inc=1, device_id={"gy": beyond("gy", dy)}, device_id_type=MESH)
        for dx, dz in around_xz:
            pl.semaphore_signal(barrier, inc=1, device_id={"gx": beyond("gx", dx), "gz": beyond("gz", dz)},
                                device_id_type=MESH)
        pl.semaphore_wait(barrier, len(NEAR) + len(around_xz))

        lane = lax.broadcasted_iota(jnp.int32, (1, LANES), 1)

        def own(level):
            return tuple(n >> level for n in shape)

        def dims(level):
            return WINDOW[level] or own(level)[:2]

        def clear_rim(level, h):
            nx, ny = dims(level)
            h.vp[0] = jnp.zeros(h.vp.shape[1:], jnp.float32)
            h.vp[nx + 1] = jnp.zeros(h.vp.shape[1:], jnp.float32)
            rim = jnp.zeros((nx, PAD, LANES), jnp.float32)
            h.vp[pl.ds(1, nx), pl.ds(0, PAD), :] = rim
            h.vp[pl.ds(1, nx), pl.ds(PAD + ny, PAD), :] = rim

        for level in range(LEVELS):
            if WINDOW[level]:
                for h in [refs.level[level].b] + refs.level[level].it:
                    clear_rim(level, h)

        def copies(level, h):
            nx, ny = dims(level)
            rows = pl.ds(PAD, round_up(ny))
            vp, zs, zr, ys, yr = h.vp, h.zs, h.zr, h.ys, h.yr
            pairs = (
                (vp.at[nx, rows], vp.at[0, rows], "gx", after),
                (vp.at[1, rows], vp.at[nx + 1, rows], "gx", before),
                (ys.at[0], yr.at[0], "gy", after),
                (ys.at[1], yr.at[1], "gy", before),
                (zs.at[0], zr.at[0], "gz", after),
                (zs.at[1], zr.at[1], "gz", before),
            )
            return [
                pltpu.make_async_remote_copy(
                    src_ref=src, dst_ref=dst, send_sem=h.send.at[i], recv_sem=h.recv.at[i],
                    device_id={axis: where[axis]}, device_id_type=MESH)
                for i, (src, dst, axis, where) in enumerate(pairs)
            ]

        def finish(level, h):
            if WINDOW[level]:
                return
            nx, ny = dims(level)
            nz = own(level)[2]
            for copy in copies(level, h):
                copy.wait()
            for x in range(nx):
                h.vp[x + 1, pl.ds(PAD - 1, 1), :] = h.yr[0, pl.ds(x, 1), :]
                h.vp[x + 1, pl.ds(PAD + ny, 1), :] = h.yr[1, pl.ds(x, 1), :]
            if level > 0:
                low, high = h.zr[0, pl.ds(0, ny), :], h.zr[1, pl.ds(0, ny), :]
                for x in range(nx):
                    plane = h.vp[x + 1, pl.ds(PAD, ny), :]
                    plane = jnp.where(lane == LANES - 1, pltpu.roll(low, LANES - 1 - x, 1), plane)
                    h.vp[x + 1, pl.ds(PAD, ny), :] = jnp.where(lane == nz, pltpu.roll(high, nz - x, 1), plane)

        def sweep(level, make, h):
            nx, ny = dims(level)
            nz = own(level)[2]
            if WINDOW[level]:
                def inside(x, carry):
                    h.vp[x + 1, pl.ds(PAD, ny), :] = make(x)
                    return carry

                lax.fori_loop(0, nx, inside, 0)
                return
            zero = jnp.zeros((ny, LANES), jnp.float32)

            def body(x, carry):
                high, low = carry
                plane = make(x)
                h.vp[x + 1, pl.ds(PAD, ny), :] = plane
                h.ys[0, pl.ds(x, 1), :] = plane[ny - 1:ny]
                h.ys[1, pl.ds(x, 1), :] = plane[0:1]
                here = lane == x
                high = jnp.where(here, pltpu.roll(plane, lax.rem(x + LANES - (nz - 1), LANES), 1), high)
                low = jnp.where(here, pltpu.roll(plane, x, 1), low)
                return high, low

            high, low = lax.fori_loop(0, nx, body, (zero, zero))
            h.zs[0, pl.ds(0, ny), :] = high
            h.zs[1, pl.ds(0, ny), :] = low
            for copy in copies(level, h):
                copy.start()

        def around(level, h, x):
            nx, ny = dims(level)
            vp = h.vp
            mid = vp[x + 1, pl.ds(PAD, ny), :]
            zm, zp = pltpu.roll(mid, 1, 1), pltpu.roll(mid, LANES - 1, 1)
            if level == 0:
                zlow, zhigh = h.zr[0], h.zr[1]
                zm = jnp.where(lane == 0, pltpu.roll(zlow, lax.rem(LANES - x, LANES), 1), zm)
                zp = jnp.where(lane == LANES - 1, pltpu.roll(zhigh, LANES - 1 - x, 1), zp)
            return (mid, vp[x, pl.ds(PAD, ny), :], vp[x + 2, pl.ds(PAD, ny), :],
                    vp[x + 1, pl.ds(PAD - 1, ny), :], vp[x + 1, pl.ds(PAD + 1, ny), :], zm, zp)

        def residual(level, h, x):
            g = refs.level[level]
            mid, xm, xp, ym, yp, zm, zp = around(level, h, x)
            total = g.sx[x] * xm + g.sx[x + 1] * xp + g.sym[x] * ym + g.syp[x] * yp + g.szm[x] * zm + g.szp[x] * zp
            return mid, source(level, x) - g.q[x] * mid + total

        def source(level, x):
            return rhs[x] if level == 0 else refs.level[level].f[x]

        def reaction(level, x):
            return coef_c[x] if level == 0 else refs.level[level].c[x]

        row_of = lax.broadcasted_iota(jnp.int32, (LANES, LANES), 0)
        col_of = lax.broadcasted_iota(jnp.int32, (LANES, LANES), 1)

        def pairing(level, wide, narrow):
            half = wide // 2
            return (half if level == 0 else half + jnp.where(wide >= 96, 64, 0)) == narrow

        def coarsen(level, get, put):
            nx, ny = dims(level)
            pair = refs.level[level].pair
            shrink = jnp.where(pairing(level, row_of, col_of), 0.125, 0.0).astype(jnp.bfloat16)

            def body(x, carry):
                pair[x, pl.ds(0, ny), :] = get(2 * x) + get(2 * x + 1)
                return carry

            lax.fori_loop(0, nx // 2, body, 0)
            for x in range(nx // 2):
                even = pair[x, pl.ds(0, ny // 2, 2), :]
                odd = pair[x, pl.ds(1, ny // 2, 2), :]
                put(x, exact_dot(even + odd, shrink))

        def refine(level, planes, get):
            pair = refs.level[level].pair
            grow = jnp.where(pairing(level, col_of, row_of), 1.0, 0.0).astype(jnp.bfloat16)
            for x in range(planes):
                wide = exact_dot(get(x), grow)
                rows = wide.shape[0]
                pair[x, pl.ds(0, rows, 2), :] = wide
                pair[x, pl.ds(1, rows, 2), :] = wide

        def store(ref):
            def put(x, plane):
                ref[x] = plane

            return put

        def block_to(h, which):
            def put(x, plane):
                mean = pltpu.roll(jnp.where(lane < 32, plane, 0.0), 32 * x, 1)
                rows = pl.ds(0, 12)
                h.block[which, rows, :] = mean if x == 0 else h.block[which, rows, :] + mean

            return put

        def near_copies(h):
            return [
                pltpu.make_async_remote_copy(
                    src_ref=h.block, dst_ref=h.near.at[3 - i], send_sem=h.near_send.at[i],
                    recv_sem=h.near_recv.at[3 - i], device_id={"gy": beyond("gy", dy)}, device_id_type=MESH)
                for i, dy in enumerate(NEAR)
            ]

        def all_copies(h):
            return [
                pltpu.make_async_remote_copy(
                    src_ref=h.column, dst_ref=h.all.at[1 - dz, place["gx"]], send_sem=h.all_send.at[1 - dz, dx],
                    recv_sem=h.all_recv.at[1 - dz, dx],
                    device_id={"gx": beyond("gx", dx), "gz": beyond("gz", dz)}, device_id_type=MESH)
                for dx, dz in around_xz
            ]

        def gather_near(h):
            for copy in near_copies(h):
                copy.start()

        def gather_all(h, arrays):
            for copy in near_copies(h):
                copy.wait()
            for k in range(arrays):
                h.column[k, pl.ds(0, 6), :] = h.near[0, k, pl.ds(6, 6), :]
                h.column[k, pl.ds(6, 12), :] = h.near[1, k, pl.ds(0, 12), :]
                h.column[k, pl.ds(18, 12), :] = h.block[k, pl.ds(0, 12), :]
                h.column[k, pl.ds(30, 12), :] = h.near[2, k, pl.ds(0, 12), :]
                h.column[k, pl.ds(42, 6), :] = h.near[3, k, pl.ds(0, 6), :]
            for copy in all_copies(h):
                copy.start()
            h.all[1, place["gx"]] = h.column[...]

        def gather_end(h):
            for copy in all_copies(h):
                copy.wait()

        def gathered(h, which, x, dx):
            left, here, right = (h.all[i, x, which] for i in range(3))
            plane = jnp.where(lane < 32, pltpu.roll(here, (LANES - 32 * dx) % LANES, 1), 0.0)
            plane = jnp.where((lane >= 32) & (lane < 64), pltpu.roll(right, (LANES + 32 - 32 * dx) % LANES, 1), plane)
            return jnp.where(lane >= 96, pltpu.roll(left, 96 - 32 * dx, 1), plane)

        def setup(level):
            g = refs.level[level]
            nx, ny = dims(level)
            nz = own(level)[2]
            half = 0.5 * 4.0 ** (LEVELS - 1 - level)
            finish(level, g.b)
            if WINDOW[level]:
                first_x = last_x = 0.0
            else:
                first_x, last_x = has_before["gx"], has_after["gx"]
                g.b.vp[0, pl.ds(PAD, ny), :] = g.b.vp[0, pl.ds(PAD, ny), :] * first_x
                g.b.vp[nx + 1, pl.ds(PAD, ny), :] = g.b.vp[nx + 1, pl.ds(PAD, ny), :] * last_x
            cells_y = own(level)[1]
            row = lax.broadcasted_iota(jnp.int32, (ny, 1), 0) + place["gy"] * cells_y - FIRST_ROW[level]
            if level == 0:
                column, used = lane, lane >= 0
            else:
                column = jnp.where(lane < 96, lane, lane - LANES)
                used = (column < 2 * nz) & (column >= -nz) if WINDOW[level] else (lane < nz)
            column = column + place["gz"] * nz
            keep_ym = jnp.where(row == 0, 0.0, 1.0)
            keep_yp = jnp.where(row == cells_y * count["gy"] - 1, 0.0, 1.0)
            keep_zm = jnp.where(column == 0, 0.0, 1.0)
            keep_zp = jnp.where(column == nz * count["gz"] - 1, 0.0, 1.0)

            def body(x, carry):
                mid, xm, xp, ym, yp, zm, zp = around(level, g.b, x)
                fxm, fxp = half * (mid + xm), half * (mid + xp)
                fym, fyp = half * (mid + ym * keep_ym), half * (mid + yp * keep_yp)
                fzm, fzp = half * (mid + zm * keep_zm), half * (mid + zp * keep_zp)
                q = reaction(level, x) + (fxm + fxp + fym + fyp + fzm + fzp)
                g.q[x] = q
                g.rq[x] = jnp.where(used, 1.0 / q, 0.0)
                g.sx[x] = fxm * jnp.where(x == 0, first_x, 1.0)
                g.sym[x] = fym * keep_ym
                g.syp[x] = fyp * keep_yp
                g.szm[x] = fzm * keep_zm
                g.szp[x] = fzp * keep_zp
                return carry

            lax.fori_loop(0, nx, body, 0)
            last = g.b.vp[nx, pl.ds(PAD, ny), :] + g.b.vp[nx + 1, pl.ds(PAD, ny), :]
            g.sx[nx] = half * last * last_x

        def planes_of(level, h):
            ny = dims(level)[1]
            return lambda x: h.vp[x + 1, pl.ds(PAD, ny), :]

        levels = refs.level
        (_, first), (carry_e, weight_r) = chebyshev(2)
        of_f, of_bc = refs.gather

        def start_down(level):
            g = levels[level]
            sweep(level, lambda x: source(level, x) * g.rq[x] * first, g.it[0])

        def go_down(level):
            g = levels[level]

            def second(x):
                mid, rest = residual(level, g.it[0], x)
                return mid * (1.0 + carry_e) + weight_r * rest * g.rq[x]

            finish(level, g.it[0])
            sweep(level, second, g.it[1])

        def leave(level, put):
            g = levels[level]
            finish(level, g.it[1])
            coarsen(level, lambda x: residual(level, g.it[1], x)[1], put)

        def go_up(level, begun, ended, put):
            g = levels[level]

            def third(x):
                mid, rest = residual(level, begun, x)
                update = first * rest * g.rq[x]
                g.e[x] = update
                return mid + update

            sweep(level, third, ended)
            finish(level, ended)

            def last(x, carry):
                mid, rest = residual(level, ended, x)
                put(x, mid + carry_e * g.e[x] + weight_r * rest * g.rq[x])
                return carry

            lax.fori_loop(0, dims(level)[0], last, 0)

        sweep(0, lambda x: coef_b[x], levels[0].b)
        coarsen(0, lambda x: coef_b[x], store(levels[1].f))
        coarsen(0, lambda x: coef_c[x], store(levels[1].c))
        sweep(1, lambda x: levels[1].f[x], levels[1].b)
        coarsen(1, lambda x: levels[1].f[x], block_to(of_bc, 0))
        coarsen(1, lambda x: levels[1].c[x], block_to(of_bc, 1))
        gather_near(of_bc)

        setup(0)
        start_down(0)
        gather_all(of_bc, 2)
        setup(1)
        go_down(0)
        gather_end(of_bc)
        for dx in range(4):
            def spread(x, carry, dx=dx):
                levels[2].b.vp[4 * x + dx + 1, pl.ds(PAD, 48), :] = gathered(of_bc, 0, x, dx)
                levels[2].c[4 * x + dx] = gathered(of_bc, 1, x, dx)
                return carry

            lax.fori_loop(0, 4, spread, 0)
        coarsen(2, planes_of(2, levels[2].b), store(levels[3].f))
        sweep(3, lambda x: levels[3].f[x], levels[3].b)
        coarsen(2, lambda x: levels[2].c[x], store(levels[3].c))
        setup(2)
        setup(3)
        leave(0, store(levels[1].f))

        start_down(1)
        go_down(1)
        leave(1, block_to(of_f, 0))
        gather_near(of_f)
        gather_all(of_f, 1)
        gather_end(of_f)
        for dx in range(4):
            def spread_f(x, carry, dx=dx):
                levels[2].f[4 * x + dx] = gathered(of_f, 0, x, dx)
                return carry

            lax.fori_loop(0, 4, spread_f, 0)

        start_down(2)
        go_down(2)
        leave(2, store(levels[3].f))

        g = levels[3]
        steps = chebyshev(COARSE_SWEEPS)

        def begin(x):
            update = source(3, x) * g.rq[x] * steps[0][1]
            g.e[x] = update
            return update

        sweep(3, begin, g.it[0])
        for step in range(1, COARSE_SWEEPS):
            def advance(x, step=step):
                mid, rest = residual(3, g.it[(step - 1) % 2], x)
                update = steps[step][0] * g.e[x] + steps[step][1] * rest * g.rq[x]
                g.e[x] = update
                return mid + update

            sweep(3, advance, g.it[step % 2])

        refine(2, 8, planes_of(3, g.it[(COARSE_SWEEPS - 1) % 2]))
        g = levels[2]
        sweep(2, lambda x: planes_of(2, g.it[1])(x) + g.pair[x // 2], g.it[0])
        go_up(2, g.it[0], g.it[1], store(g.f))

        g = levels[1]
        start_x = place["gx"] * own(2)[0]
        refine(1, 6, lambda x: levels[2].f[jnp.clip(start_x + x - 1, 0, 15), pl.ds(16, 16), :])
        rows = pl.ds(PAD - 1, 26)
        for x in range(10):
            g.it[2].vp[x, rows, :] = g.it[1].vp[x, rows, :] + g.pair[(x + 1) // 2, pl.ds(3, 26), :]
        go_up(1, g.it[2], g.it[3], store(g.f))

        g = levels[0]
        refine(0, 8, lambda x: levels[1].f[x])
        sweep(0, lambda x: planes_of(0, g.it[1])(x) + g.pair[x // 2], g.it[2])
        finish(0, g.it[2])
        go_up(0, g.it[2], g.it[3], store(out))

    return kernel


class Plan:
    def __init__(self, shape):
        self.shapes = []
        self.tree = Names()
        self.tree.level = []
        for level in range(LEVELS):
            nx, ny = WINDOW[level] or tuple(n >> level for n in shape)[:2]
            g = Names()

            def planes(n, ny=ny):
                return self.add(pltpu.VMEM((n, ny, LANES), jnp.float32))

            def halo(exchanged, nx=nx, ny=ny):
                h = Names()
                h.vp = self.add(pltpu.VMEM((nx + 2, round_up(ny) + 2 * PAD, LANES), jnp.float32))
                if exchanged:
                    for name, rows in (("zs", ny), ("zr", ny), ("ys", nx), ("yr", nx)):
                        setattr(h, name, self.add(pltpu.VMEM((2, round_up(rows), LANES), jnp.float32)))
                    h.send = self.add(pltpu.SemaphoreType.DMA((6,)))
                    h.recv = self.add(pltpu.SemaphoreType.DMA((6,)))
                return h

            exchanged = WINDOW[level] is None
            g.b = halo(exchanged)
            g.sx = planes(nx + 1)
            for name in ("sym", "syp", "szm", "szp", "q", "rq", "e"):
                setattr(g, name, planes(nx))
            if level > 0:
                g.f = planes(nx)
                g.c = planes(nx)
            if level == 1:
                g.pair = self.add(pltpu.VMEM((nx // 2 + 2, 32, LANES), jnp.float32))
            elif level < LEVELS - 1:
                g.pair = planes(nx // 2)
            g.it = [halo(exchanged) for _ in range(4 if exchanged else 2)]
            self.tree.level.append(g)
        self.tree.gather = [self.gathered(1), self.gathered(2)]

    def gathered(self, arrays):
        h = Names()
        h.block = self.add(pltpu.VMEM((arrays, 16, LANES), jnp.float32))
        h.near = self.add(pltpu.VMEM((4, arrays, 16, LANES), jnp.float32))
        h.column = self.add(pltpu.VMEM((arrays, 48, LANES), jnp.float32))
        h.all = self.add(pltpu.VMEM((3, 4, arrays, 48, LANES), jnp.float32))
        h.near_send = self.add(pltpu.SemaphoreType.DMA((4,)))
        h.near_recv = self.add(pltpu.SemaphoreType.DMA((4,)))
        h.all_send = self.add(pltpu.SemaphoreType.DMA((3, 4)))
        h.all_recv = self.add(pltpu.SemaphoreType.DMA((3, 4)))
        return h

    def add(self, shape):
        self.shapes.append(shape)
        return len(self.shapes) - 1

    def unpack(self, refs):
        def walk(node):
            if isinstance(node, int):
                return refs[node]
            if isinstance(node, list):
                return [walk(item) for item in node]
            result = Names()
            for name, item in vars(node).items():
                setattr(result, name, walk(item))
            return result

        return walk(self.tree)


def solution(mesh):
    sizes = dict(mesh.shape)

    def local(rhs, coef_b, coef_c):
        shape = rhs.shape
        plan = Plan(shape)
        return pl.pallas_call(
            make_kernel(shape, sizes, plan),
            out_shape=jax.ShapeDtypeStruct(shape, jnp.float32),
            in_specs=[pl.BlockSpec(memory_space=pltpu.VMEM)] * 3,
            out_specs=pl.BlockSpec(memory_space=pltpu.VMEM),
            scratch_shapes=plan.shapes,
            compiler_params=pltpu.CompilerParams(
                collective_id=0, has_side_effects=True, vmem_limit_bytes=40 * 2**20),
        )(rhs, coef_b, coef_c)

    return jax.shard_map(
        local,
        mesh=mesh,
        in_specs=(P(*AXES),) * 3,
        out_specs=P(*AXES),
        check_vma=False,
    )
```

time: 99.7 us -> 84.6 us (0.85)
  Pallas kernels: 95.8 us -> 80.7 us
    pallas_call x1, Pallas kernels: 95.8 us -> 80.7 us  [local(): pl.pallas_call(make_kernel(shape, sizes, plan), out_shape=jax.ShapeDtypeS...]
where the time goes in v2:
time: 84.6 us; the launch traced here: 84.5 us
  Pallas kernels  80.7 us (95%)
  local copies, waits for them, and re-layouts  3.73 us (4%)
    pallas_call x1, Pallas kernels, local(): pl.pallas_call(make_kernel(shape, sizes, plan), out_shape=jax.ShapeDtypeS...  80.7 us
    unnamed x7, local copies, waits for them, and re-layouts  3.73 us

profile of v2, /device:TPU:1, one launch (start us, length us, event | category | flops | bytes accessed | tf_op | source)
XLA Modules:
  0.0 84.5 jit_solution(10659663789815770751)
XLA Ops:
  0.0 0.0 copy-start
  0.0 1.0 %copy-done = f32[16,48,128]{2,1,0:T(8,128)S(1)} copy-done((f32[16,48,128]{2,1,0:T(8,128)S(1)}, f32[16,48,128]{2,1,0:T(8,128)}, u32[]{:S(2)}) %copy-start) | copy-done | bytes 393240
  1.0 0.0 copy-start.1
  1.0 1.0 %copy-done.1 = f32[16,48,128]{2,1,0:T(8,128)S(1)} copy-done((f32[16,48,128]{2,1,0:T(8,128)S(1)}, f32[16,48,128]{2,1,0:T(8,128)}, u32[]{:S(2)}) %copy-start.1) | copy-done | bytes 393240
  2.0 0.0 copy-start.2
  2.0 1.0 %copy-done.2 = f32[16,48,128]{2,1,0:T(8,128)S(1)} copy-done((f32[16,48,128]{2,1,0:T(8,128)S(1)}, f32[16,48,128]{2,1,0:T(8,128)}, u32[]{:S(2)}) %copy-start.2) | copy-done | bytes 393240
  3.0 80.7 %shard_map.37 = f32[16,48,128]{2,1,0:T(8,128)S(1)} custom-call(f32[16,48,128]{2,1,0:T(8,128)S(1)} %copy-done, f32[16,48,128]{2,1,0:T(8,128)S(1)} %copy-done.1, f32[16,48,128]{2,1,0:T(8,128)S(1)} %copy-done.2), custom_call_target="tpu_custom_call" | custom-call | tf_op jit(solution)/shard_map/pallas_call | solution.py:524
  83.7 0.7 copy.5
Async XLA Ops:
  0.0 1.0 %copy-start = (f32[16,48,128]{2,1,0:T(8,128)S(1)}, f32[16,48,128]{2,1,0:T(8,128)}, u32[]{:S(2)}) copy-start(f32[16,48,128]{2,1,0:T(8,128)} %rhs.1) | copy-start | bytes 1179652
  1.0 1.0 %copy-start.1 = (f32[16,48,128]{2,1,0:T(8,128)S(1)}, f32[16,48,128]{2,1,0:T(8,128)}, u32[]{:S(2)}) copy-start(f32[16,48,128]{2,1,0:T(8,128)} %coef_b.1) | copy-start | bytes 1179652
  2.0 1.0 %copy-start.2 = (f32[16,48,128]{2,1,0:T(8,128)S(1)}, f32[16,48,128]{2,1,0:T(8,128)}, u32[]{:S(2)}) copy-start(f32[16,48,128]{2,1,0:T(8,128)} %coef_c.1) | copy-start | bytes 1179652

commit v3 on v2

--- a/solution.py
+++ b/solution.py
@@ -47,6 +47,7 @@
 WINDOW = (None, None, (16, 48), (8, 24))
 FIRST_ROW = (0, 0, 18, 9)
 NEAR = (-2, -1, 1, 2)
+TOGETHER = 8
 
 
 def make_kernel(shape, sizes, plan):
@@ -130,22 +131,41 @@
                     plane = jnp.where(lane == LANES - 1, pltpu.roll(low, LANES - 1 - x, 1), plane)
                     h.vp[x + 1, pl.ds(PAD, ny), :] = jnp.where(lane == nz, pltpu.roll(high, nz - x, 1), plane)
 
+        def planes(n, make, put, carry=None):
+            step = min(n, TOGETHER)
+
+            def body(i, carry):
+                made = [make(i * step + k) for k in range(step)]
+                for k in range(step):
+                    if carry is None:
+                        put(i * step + k, made[k])
+                    else:
+                        carry = put(i * step + k, made[k], carry)
+                return carry
+
+            if carry is not None:
+                return lax.fori_loop(0, n // step, body, carry)
+
+            def plain(i, zero):
+                body(i, None)
+                return zero
+
+            lax.fori_loop(0, n // step, plain, 0)
+
         def sweep(level, make, h):
             nx, ny = dims(level)
             nz = own(level)[2]
+            def keep(x, plane):
+                h.vp[x + 1, pl.ds(PAD, ny), :] = plane
+
             if WINDOW[level]:
-                def inside(x, carry):
-                    h.vp[x + 1, pl.ds(PAD, ny), :] = make(x)
-                    return carry
-
-                lax.fori_loop(0, nx, inside, 0)
+                planes(nx, make, keep)
                 return
             zero = jnp.zeros((ny, LANES), jnp.float32)
 
-            def body(x, carry):
+            def pack(x, plane, carry):
+                keep(x, plane)
                 high, low = carry
-                plane = make(x)
-                h.vp[x + 1, pl.ds(PAD, ny), :] = plane
                 h.ys[0, pl.ds(x, 1), :] = plane[ny - 1:ny]
                 h.ys[1, pl.ds(x, 1), :] = plane[0:1]
                 here = lane == x
@@ -153,7 +173,7 @@
                 low = jnp.where(here, pltpu.roll(plane, x, 1), low)
                 return high, low
 
-            high, low = lax.fori_loop(0, nx, body, (zero, zero))
+            high, low = planes(nx, make, pack, (zero, zero))
             h.zs[0, pl.ds(0, ny), :] = high
             h.zs[1, pl.ds(0, ny), :] = low
             for copy in copies(level, h):
@@ -195,11 +215,10 @@
             pair = refs.level[level].pair
             shrink = jnp.where(pairing(level, row_of, col_of), 0.125, 0.0).astype(jnp.bfloat16)
 
-            def body(x, carry):
-                pair[x, pl.ds(0, ny), :] = get(2 * x) + get(2 * x + 1)
-                return carry
-
-            lax.fori_loop(0, nx // 2, body, 0)
+            def put_pair(x, plane):
+                pair[x, pl.ds(0, ny), :] = plane
+
+            planes(nx // 2, lambda x: get(2 * x) + get(2 * x + 1), put_pair)
             for x in range(nx // 2):
                 even = pair[x, pl.ds(0, ny // 2, 2), :]
                 odd = pair[x, pl.ds(1, ny // 2, 2), :]
@@ -297,22 +316,20 @@
             keep_zm = jnp.where(column == 0, 0.0, 1.0)
             keep_zp = jnp.where(column == nz * count["gz"] - 1, 0.0, 1.0)
 
-            def body(x, carry):
+            def make(x):
                 mid, xm, xp, ym, yp, zm, zp = around(level, g.b, x)
                 fxm, fxp = half * (mid + xm), half * (mid + xp)
                 fym, fyp = half * (mid + ym * keep_ym), half * (mid + yp * keep_yp)
                 fzm, fzp = half * (mid + zm * keep_zm), half * (mid + zp * keep_zp)
                 q = reaction(level, x) + (fxm + fxp + fym + fyp + fzm + fzp)
-                g.q[x] = q
-                g.rq[x] = jnp.where(used, 1.0 / q, 0.0)
-                g.sx[x] = fxm * jnp.where(x == 0, first_x, 1.0)
-                g.sym[x] = fym * keep_ym
-                g.syp[x] = fyp * keep_yp
-                g.szm[x] = fzm * keep_zm
-                g.szp[x] = fzp * keep_zp
-                return carry
-
-            lax.fori_loop(0, nx, body, 0)
+                return (q, jnp.where(used, 1.0 / q, 0.0), fxm * jnp.where(x == 0, first_x, 1.0),
+                        fym * keep_ym, fyp * keep_yp, fzm * keep_zm, fzp * keep_zp)
+
+            def put(x, values):
+                for name, value in zip(("q", "rq", "sx", "sym", "syp", "szm", "szp"), values):
+                    getattr(g, name)[x] = value
+
+            planes(nx, make, put)
             last = g.b.vp[nx, pl.ds(PAD, ny), :] + g.b.vp[nx + 1, pl.ds(PAD, ny), :]
             g.sx[nx] = half * last * last_x
 
@@ -355,12 +372,11 @@
             sweep(level, third, ended)
             finish(level, ended)
 
-            def last(x, carry):
+            def last(x):
                 mid, rest = residual(level, ended, x)
-                put(x, mid + carry_e * g.e[x] + weight_r * rest * g.rq[x])
-                return carry
-
-            lax.fori_loop(0, dims(level)[0], last, 0)
+                return mid + carry_e * g.e[x] + weight_r * rest * g.rq[x]
+
+            planes(dims(level)[0], last, put)
 
         sweep(0, lambda x: coef_b[x], levels[0].b)
         coarsen(0, lambda x: coef_b[x], store(levels[1].f))

time: 84.6 us -> 63.6 us (0.75)
  Pallas kernels: 80.7 us -> 59.7 us
    pallas_call x1, Pallas kernels: 80.7 us -> 59.7 us  [local(): pl.pallas_call(make_kernel(shape, sizes, plan), out_shape=jax.ShapeDtypeS...]
where the time goes in v3:
time: 63.6 us; the launch traced here: 63.4 us
  Pallas kernels  59.7 us (94%)
  local copies, waits for them, and re-layouts  3.73 us (6%)
    pallas_call x1, Pallas kernels, local(): pl.pallas_call(make_kernel(shape, sizes, plan), out_shape=jax.ShapeDtypeS...  59.7 us
    unnamed x7, local copies, waits for them, and re-layouts  3.73 us

profile of v3, /device:TPU:1, one launch (start us, length us, event | category | flops | bytes accessed | tf_op | source)
XLA Modules:
  0.0 63.4 jit_solution(6493625571257250249)
XLA Ops:
  0.0 0.0 copy-start
  0.0 1.0 %copy-done = f32[16,48,128]{2,1,0:T(8,128)S(1)} copy-done((f32[16,48,128]{2,1,0:T(8,128)S(1)}, f32[16,48,128]{2,1,0:T(8,128)}, u32[]{:S(2)}) %copy-start) | copy-done | bytes 393240
  1.0 0.0 copy-start.1
  1.0 1.0 %copy-done.1 = f32[16,48,128]{2,1,0:T(8,128)S(1)} copy-done((f32[16,48,128]{2,1,0:T(8,128)S(1)}, f32[16,48,128]{2,1,0:T(8,128)}, u32[]{:S(2)}) %copy-start.1) | copy-done | bytes 393240
  2.0 0.0 copy-start.2
  2.0 1.0 %copy-done.2 = f32[16,48,128]{2,1,0:T(8,128)S(1)} copy-done((f32[16,48,128]{2,1,0:T(8,128)S(1)}, f32[16,48,128]{2,1,0:T(8,128)}, u32[]{:S(2)}) %copy-start.2) | copy-done | bytes 393240
  3.0 59.7 %shard_map.37 = f32[16,48,128]{2,1,0:T(8,128)S(1)} custom-call(f32[16,48,128]{2,1,0:T(8,128)S(1)} %copy-done, f32[16,48,128]{2,1,0:T(8,128)S(1)} %copy-done.1, f32[16,48,128]{2,1,0:T(8,128)S(1)} %copy-done.2), custom_call_target="tpu_custom_call" | custom-call | tf_op jit(solution)/shard_map/pallas_call | solution.py:540
  62.7 0.7 %copy.5 = f32[16,48,128]{2,1,0:T(8,128)} copy(f32[16,48,128]{2,1,0:T(8,128)S(1)} %shard_map.37) | data formatting | bytes 786432
Async XLA Ops:
  0.0 1.0 %copy-start = (f32[16,48,128]{2,1,0:T(8,128)S(1)}, f32[16,48,128]{2,1,0:T(8,128)}, u32[]{:S(2)}) copy-start(f32[16,48,128]{2,1,0:T(8,128)} %rhs.1) | copy-start | bytes 1179652
  1.0 1.0 %copy-start.1 = (f32[16,48,128]{2,1,0:T(8,128)S(1)}, f32[16,48,128]{2,1,0:T(8,128)}, u32[]{:S(2)}) copy-start(f32[16,48,128]{2,1,0:T(8,128)} %coef_b.1) | copy-start | bytes 1179652
  2.0 1.0 %copy-start.2 = (f32[16,48,128]{2,1,0:T(8,128)S(1)}, f32[16,48,128]{2,1,0:T(8,128)}, u32[]{:S(2)}) copy-start(f32[16,48,128]{2,1,0:T(8,128)} %coef_c.1) | copy-start | bytes 1179652

commit v4 on v3

--- a/solution.py
+++ b/solution.py
@@ -44,8 +44,8 @@
     return total + jnp.dot(high, matrix, preferred_element_type=jnp.float32)
 
 
-WINDOW = (None, None, (16, 48), (8, 24))
-FIRST_ROW = (0, 0, 18, 9)
+WINDOW = (None, (16, 40), (16, 48), (8, 24))
+FIRST_ROW = (0, 8, 18, 9)
 NEAR = (-2, -1, 1, 2)
 TOGETHER = 8
 
@@ -62,22 +62,26 @@
 
         after = {axis: beyond(axis, 1) for axis in AXES}
         before = {axis: beyond(axis, -1) for axis in AXES}
-        has_before = {a: jnp.where(place[a] > 0, 1.0, 0.0).astype(jnp.float32) for a in AXES}
-        has_after = {a: jnp.where(place[a] < count[a] - 1, 1.0, 0.0).astype(jnp.float32) for a in AXES}
-        around_xz = [(dx, dz) for dx in range(4) for dz in (-1, 0, 1) if (dx, dz) != (0, 0)]
-
-        barrier = pltpu.get_barrier_semaphore()
-        for dy in NEAR:
-            pl.semaphore_signal(barrier, inc=1, device_id={"gy": beyond("gy", dy)}, device_id_type=MESH)
-        for dx, dz in around_xz:
-            pl.semaphore_signal(barrier, inc=1, device_id={"gx": beyond("gx", dx), "gz": beyond("gz", dz)},
-                                device_id_type=MESH)
-        pl.semaphore_wait(barrier, len(NEAR) + len(around_xz))
-
-        lane = lax.broadcasted_iota(jnp.int32, (1, LANES), 1)
-
         def own(level):
             return tuple(n >> level for n in shape)
+
+        def first_plane(level):
+            if level > 1:
+                return 0
+            return place["gx"] * own(level)[0] - (4 if level == 1 else 0)
+
+        sides = (-1, 0, 1)
+        around_all = [(dx, dy, dz) for dx in sides for dy in sides for dz in sides if (dx, dy, dz) != (0, 0, 0)]
+        around_xz = [(dx, dz) for dx in range(4) for dz in (-1, 0, 1) if (dx, dz) != (0, 0)]
+
+        barrier = pltpu.get_barrier_semaphore()
+        partners = [offset for offset in around_all if sum(map(abs, offset)) == 1]
+        for offset in partners:
+            pl.semaphore_signal(barrier, inc=1, device_id={a: beyond(a, d) for a, d in zip(AXES, offset)},
+                                device_id_type=MESH)
+        pl.semaphore_wait(barrier, len(partners))
+
+        lane = lax.broadcasted_iota(jnp.int32, (1, LANES), 1)
 
         def dims(level):
             return WINDOW[level] or own(level)[:2]
@@ -118,18 +122,11 @@
             if WINDOW[level]:
                 return
             nx, ny = dims(level)
-            nz = own(level)[2]
             for copy in copies(level, h):
                 copy.wait()
             for x in range(nx):
                 h.vp[x + 1, pl.ds(PAD - 1, 1), :] = h.yr[0, pl.ds(x, 1), :]
                 h.vp[x + 1, pl.ds(PAD + ny, 1), :] = h.yr[1, pl.ds(x, 1), :]
-            if level > 0:
-                low, high = h.zr[0, pl.ds(0, ny), :], h.zr[1, pl.ds(0, ny), :]
-                for x in range(nx):
-                    plane = h.vp[x + 1, pl.ds(PAD, ny), :]
-                    plane = jnp.where(lane == LANES - 1, pltpu.roll(low, LANES - 1 - x, 1), plane)
-                    h.vp[x + 1, pl.ds(PAD, ny), :] = jnp.where(lane == nz, pltpu.roll(high, nz - x, 1), plane)
 
         def planes(n, make, put, carry=None):
             step = min(n, TOGETHER)
@@ -210,28 +207,94 @@
             half = wide // 2
             return (half if level == 0 else half + jnp.where(wide >= 96, 64, 0)) == narrow
 
-        def coarsen(level, get, put):
-            nx, ny = dims(level)
+        def coarsen(level, count_x, get, put=None):
             pair = refs.level[level].pair
             shrink = jnp.where(pairing(level, row_of, col_of), 0.125, 0.0).astype(jnp.bfloat16)
 
             def put_pair(x, plane):
-                pair[x, pl.ds(0, ny), :] = plane
-
-            planes(nx // 2, lambda x: get(2 * x) + get(2 * x + 1), put_pair)
-            for x in range(nx // 2):
-                even = pair[x, pl.ds(0, ny // 2, 2), :]
-                odd = pair[x, pl.ds(1, ny // 2, 2), :]
-                put(x, exact_dot(even + odd, shrink))
-
-        def refine(level, planes, get):
+                pair[x, pl.ds(0, plane.shape[0]), :] = plane
+
+            planes(count_x // 2, lambda x: get(2 * x) + get(2 * x + 1), put_pair)
+            half = (own(1)[1] // 2) if level == 1 else dims(level)[1] // 2
+            made = []
+            for x in range(count_x // 2):
+                even = pair[x, pl.ds(0, half, 2), :]
+                odd = pair[x, pl.ds(1, half, 2), :]
+                made.append(exact_dot(even + odd, shrink))
+            if put is not None:
+                for x, plane in enumerate(made):
+                    put(x, plane)
+            return made
+
+        def refine(level, count_x, get):
             pair = refs.level[level].pair
             grow = jnp.where(pairing(level, col_of, row_of), 1.0, 0.0).astype(jnp.bfloat16)
-            for x in range(planes):
+            for x in range(count_x):
                 wide = exact_dot(get(x), grow)
                 rows = wide.shape[0]
                 pair[x, pl.ds(0, rows, 2), :] = wide
                 pair[x, pl.ds(1, rows, 2), :] = wide
+
+        def block_parts(h, which, made):
+            rows = own(1)[1]
+            outer = jnp.zeros((rows, LANES), jnp.float32)
+            for x, plane in enumerate(made):
+                if x % 2:
+                    h.pairs[which, x // 2] = made[x - 1] + pltpu.roll(plane, 64, 1)
+                low = (lane >= 8 * x) & (lane < 8 * x + 8)
+                high = (lane >= 64 + 8 * x) & (lane < 72 + 8 * x)
+                outer = jnp.where(low, pltpu.roll(plane, 8 * x, 1), outer)
+                outer = jnp.where(high, pltpu.roll(plane, 8 * x + 8, 1), outer)
+            h.outer[which] = outer
+
+        def part_copies(h, deep):
+            every = []
+            for i, (dx, dy, dz) in enumerate(around_all):
+                rows = {-1: pl.ds(0, 8), 0: pl.ds(0, own(1)[1]), 1: pl.ds(own(1)[1] - 8, 8)}[dy]
+                pairs = {-1: pl.ds(0, deep), 0: pl.ds(0, 4), 1: pl.ds(4 - deep, deep)}[dx]
+                every_array = slice(None)
+                if dz == 0:
+                    src = h.pairs.at[every_array, pairs, rows]
+                    dst = h.pairs_in.at[1 - dx, 1 - dy, every_array, pairs, rows]
+                else:
+                    src = h.outer.at[every_array, rows]
+                    dst = h.outer_in.at[1 - dx, 1 - dy, (1 - dz) // 2, every_array, rows]
+                every.append(pltpu.make_async_remote_copy(
+                    src_ref=src, dst_ref=dst, send_sem=h.send.at[i], recv_sem=h.recv.at[i],
+                    device_id={a: beyond(a, d) for a, d in zip(AXES, (dx, dy, dz))}, device_id_type=MESH))
+            return every
+
+        def parts_start(h, deep):
+            for copy in part_copies(h, deep):
+                copy.start()
+
+        def parts_end(h, deep):
+            for copy in part_copies(h, deep):
+                copy.wait()
+
+        def part_plane(h, which, plane):
+            x = plane + 4
+            dx, x = x // 8 - 1, x % 8
+            rows_own = own(1)[1]
+            pieces = []
+            for dy, rows in ((-1, pl.ds(rows_own - 8, 8)), (0, pl.ds(0, rows_own)), (1, pl.ds(0, 8))):
+                if (dx, dy) == (0, 0):
+                    piece = h.pairs[which, x // 2, rows, :]
+                else:
+                    piece = h.pairs_in[1 + dx, 1 + dy, which, x // 2, rows, :]
+                left = h.outer_in[1 + dx, 1 + dy, 0, which, rows, :]
+                right = h.outer_in[1 + dx, 1 + dy, 1, which, rows, :]
+                if x % 2:
+                    piece = pltpu.roll(piece, 64, 1)
+                piece = jnp.where(lane < 64, piece, 0.0)
+                piece = jnp.where((lane >= 64) & (lane < 72), pltpu.roll(right, 64 - 8 * x, 1), piece)
+                pieces.append(jnp.where(lane >= 120, pltpu.roll(left, (56 - 8 * x) % LANES, 1), piece))
+            return pieces
+
+        def put_pieces(ref, index, first, pieces):
+            for piece in pieces:
+                ref[index, pl.ds(first, piece.shape[0]), :] = piece
+                first += piece.shape[0]
 
         def store(ref):
             def put(x, plane):
@@ -297,19 +360,15 @@
             nz = own(level)[2]
             half = 0.5 * 4.0 ** (LEVELS - 1 - level)
             finish(level, g.b)
-            if WINDOW[level]:
-                first_x = last_x = 0.0
-            else:
-                first_x, last_x = has_before["gx"], has_after["gx"]
-                g.b.vp[0, pl.ds(PAD, ny), :] = g.b.vp[0, pl.ds(PAD, ny), :] * first_x
-                g.b.vp[nx + 1, pl.ds(PAD, ny), :] = g.b.vp[nx + 1, pl.ds(PAD, ny), :] * last_x
+            start_x, cells_x = first_plane(level), own(level)[0] * count["gx"]
             cells_y = own(level)[1]
             row = lax.broadcasted_iota(jnp.int32, (ny, 1), 0) + place["gy"] * cells_y - FIRST_ROW[level]
             if level == 0:
                 column, used = lane, lane >= 0
             else:
                 column = jnp.where(lane < 96, lane, lane - LANES)
-                used = (column < 2 * nz) & (column >= -nz) if WINDOW[level] else (lane < nz)
+                reach = 8 if level == 1 else nz
+                used = (column < nz + reach) & (column >= -reach)
             column = column + place["gz"] * nz
             keep_ym = jnp.where(row == 0, 0.0, 1.0)
             keep_yp = jnp.where(row == cells_y * count["gy"] - 1, 0.0, 1.0)
@@ -318,11 +377,13 @@
 
             def make(x):
                 mid, xm, xp, ym, yp, zm, zp = around(level, g.b, x)
-                fxm, fxp = half * (mid + xm), half * (mid + xp)
+                keep_xm = jnp.where((start_x + x == 0) | (start_x + x == cells_x), 0.0, 1.0)
+                keep_xp = jnp.where(start_x + x == cells_x - 1, 0.0, 1.0)
+                fxm, fxp = half * (mid + xm * keep_xm), half * (mid + xp * keep_xp)
                 fym, fyp = half * (mid + ym * keep_ym), half * (mid + yp * keep_yp)
                 fzm, fzp = half * (mid + zm * keep_zm), half * (mid + zp * keep_zp)
                 q = reaction(level, x) + (fxm + fxp + fym + fyp + fzm + fzp)
-                return (q, jnp.where(used, 1.0 / q, 0.0), fxm * jnp.where(x == 0, first_x, 1.0),
+                return (q, jnp.where(used, 1.0 / q, 0.0), fxm * keep_xm,
                         fym * keep_ym, fyp * keep_yp, fzm * keep_zm, fzp * keep_zp)
 
             def put(x, values):
@@ -331,7 +392,7 @@
 
             planes(nx, make, put)
             last = g.b.vp[nx, pl.ds(PAD, ny), :] + g.b.vp[nx + 1, pl.ds(PAD, ny), :]
-            g.sx[nx] = half * last * last_x
+            g.sx[nx] = half * last * jnp.where(start_x + nx == cells_x, 0.0, 1.0)
 
         def planes_of(level, h):
             ny = dims(level)[1]
@@ -355,10 +416,13 @@
             finish(level, g.it[0])
             sweep(level, second, g.it[1])
 
-        def leave(level, put):
+        def leave(level, put=None):
             g = levels[level]
             finish(level, g.it[1])
-            coarsen(level, lambda x: residual(level, g.it[1], x)[1], put)
+            if level == 1:
+                rows = slice(FIRST_ROW[1], FIRST_ROW[1] + own(1)[1])
+                return coarsen(1, own(1)[0], lambda x: residual(1, g.it[1], x + 4)[1][rows], put)
+            return coarsen(level, dims(level)[0], lambda x: residual(level, g.it[1], x)[1], put)
 
         def go_up(level, begun, ended, put):
             g = levels[level]
@@ -378,19 +442,34 @@
 
             planes(dims(level)[0], last, put)
 
+        parts_f, parts_bc = refs.parts
+        own_planes = own(0)[0]
         sweep(0, lambda x: coef_b[x], levels[0].b)
-        coarsen(0, lambda x: coef_b[x], store(levels[1].f))
-        coarsen(0, lambda x: coef_c[x], store(levels[1].c))
-        sweep(1, lambda x: levels[1].f[x], levels[1].b)
-        coarsen(1, lambda x: levels[1].f[x], block_to(of_bc, 0))
-        coarsen(1, lambda x: levels[1].c[x], block_to(of_bc, 1))
-        gather_near(of_bc)
+        made_b = coarsen(0, own_planes, lambda x: coef_b[x])
+        block_parts(parts_bc, 0, made_b)
+        made_c = coarsen(0, own_planes, lambda x: coef_c[x])
+        block_parts(parts_bc, 1, made_c)
+        for which, made in enumerate((made_b, made_c)):
+            for x, plane in enumerate(made):
+                levels[1].e[x, pl.ds(0, own(1)[1]), :] = plane
+            coarsen(1, own(1)[0], lambda x: levels[1].e[x, pl.ds(0, own(1)[1]), :], block_to(of_bc, which))
 
         setup(0)
         start_down(0)
+        gather_near(of_bc)
+        go_down(0)
+        parts_start(parts_bc, 3)
         gather_all(of_bc, 2)
+
+        block_parts(parts_f, 0, leave(0))
+        parts_start(parts_f, 2)
+
+        parts_end(parts_bc, 3)
+        for w in range(-1, 17):
+            put_pieces(levels[1].b.vp, w + 1, PAD, part_plane(parts_bc, 0, w))
+            if 0 <= w < 16:
+                put_pieces(levels[1].c, w, 0, part_plane(parts_bc, 1, w))
         setup(1)
-        go_down(0)
         gather_end(of_bc)
         for dx in range(4):
             def spread(x, carry, dx=dx):
@@ -399,13 +478,15 @@
                 return carry
 
             lax.fori_loop(0, 4, spread, 0)
-        coarsen(2, planes_of(2, levels[2].b), store(levels[3].f))
+        coarsen(2, 16, planes_of(2, levels[2].b), store(levels[3].f))
         sweep(3, lambda x: levels[3].f[x], levels[3].b)
-        coarsen(2, lambda x: levels[2].c[x], store(levels[3].c))
+        coarsen(2, 16, lambda x: levels[2].c[x], store(levels[3].c))
         setup(2)
         setup(3)
-        leave(0, store(levels[1].f))
-
+
+        parts_end(parts_f, 2)
+        for w in range(16):
+            put_pieces(levels[1].f, w, 0, part_plane(parts_f, 0, w))
         start_down(1)
         go_down(1)
         leave(1, block_to(of_f, 0))
@@ -447,18 +528,29 @@
         go_up(2, g.it[0], g.it[1], store(g.f))
 
         g = levels[1]
-        start_x = place["gx"] * own(2)[0]
-        refine(1, 6, lambda x: levels[2].f[jnp.clip(start_x + x - 1, 0, 15), pl.ds(16, 16), :])
-        rows = pl.ds(PAD - 1, 26)
-        for x in range(10):
-            g.it[2].vp[x, rows, :] = g.it[1].vp[x, rows, :] + g.pair[(x + 1) // 2, pl.ds(3, 26), :]
-        go_up(1, g.it[2], g.it[3], store(g.f))
+        start_x = place["gx"] * own(2)[0] - 2
+        refine(1, 8, lambda x: levels[2].f[jnp.clip(start_x + x, 0, 15), pl.ds(14, 20), :])
+        sweep(1, lambda x: planes_of(1, g.it[1])(x) + g.pair[x // 2], g.it[0])
+        go_up(1, g.it[0], g.it[1], store(g.f))
 
         g = levels[0]
-        refine(0, 8, lambda x: levels[1].f[x])
-        sweep(0, lambda x: planes_of(0, g.it[1])(x) + g.pair[x // 2], g.it[2])
-        finish(0, g.it[2])
-        go_up(0, g.it[2], g.it[3], store(out))
+        refine(0, 10, lambda x: levels[1].f[x + 3])
+        begun = g.it[2]
+        for x in range(18):
+            begun.vp[x] = g.it[1].vp[x] + g.pair[(x + 1) // 2, pl.ds(8, 64), :]
+        own_rows = own(1)[1]
+        edges = [jnp.zeros((own_rows, LANES), jnp.float32)] * 2
+        for x in range(8):
+            plane = levels[1].f[x + 4, pl.ds(8, own_rows), :]
+            for side, column in enumerate((LANES - 1, 64)):
+                for target in (2 * x, 2 * x + 1):
+                    moved = pltpu.roll(plane, (target - column) % LANES, 1)
+                    edges[side] = jnp.where(lane == target, moved, edges[side])
+        for side in range(2):
+            g.edge[side, pl.ds(0, own_rows, 2), :] = edges[side]
+            g.edge[side, pl.ds(1, own_rows, 2), :] = edges[side]
+            begun.zr[side] = g.it[1].zr[side] + g.edge[side]
+        go_up(0, begun, g.it[3], store(out))
 
     return kernel
 
@@ -493,13 +585,25 @@
             if level > 0:
                 g.f = planes(nx)
                 g.c = planes(nx)
-            if level == 1:
-                g.pair = self.add(pltpu.VMEM((nx // 2 + 2, 32, LANES), jnp.float32))
+            if level == 0:
+                g.pair = self.add(pltpu.VMEM((10, 80, LANES), jnp.float32))
+                g.edge = planes(2)
             elif level < LEVELS - 1:
                 g.pair = planes(nx // 2)
             g.it = [halo(exchanged) for _ in range(4 if exchanged else 2)]
             self.tree.level.append(g)
         self.tree.gather = [self.gathered(1), self.gathered(2)]
+        self.tree.parts = [self.parted(1, shape[1] // 2), self.parted(2, shape[1] // 2)]
+
+    def parted(self, arrays, rows):
+        h = Names()
+        h.pairs = self.add(pltpu.VMEM((arrays, 4, rows, LANES), jnp.float32))
+        h.outer = self.add(pltpu.VMEM((arrays, rows, LANES), jnp.float32))
+        h.pairs_in = self.add(pltpu.VMEM((3, 3, arrays, 4, rows, LANES), jnp.float32))
+        h.outer_in = self.add(pltpu.VMEM((3, 3, 2, arrays, rows, LANES), jnp.float32))
+        h.send = self.add(pltpu.SemaphoreType.DMA((26,)))
+        h.recv = self.add(pltpu.SemaphoreType.DMA((26,)))
+        return h
 
     def gathered(self, arrays):
         h = Names()

time: 63.6 us -> 60.7 us (0.954)
  Pallas kernels: 59.7 us -> 56.8 us
    pallas_call x1, Pallas kernels: 59.7 us -> 56.8 us  [local(): pl.pallas_call(make_kernel(shape, sizes, plan), out_shape=jax.ShapeDtypeS...]
where the time goes in v4:
time: 60.7 us; the launch traced here: 60.5 us
  Pallas kernels  56.8 us (94%)
  local copies, waits for them, and re-layouts  3.73 us (6%)
    pallas_call x1, Pallas kernels, local(): pl.pallas_call(make_kernel(shape, sizes, plan), out_shape=jax.ShapeDtypeS...  56.8 us
    unnamed x7, local copies, waits for them, and re-layouts  3.73 us

profile of v4, /device:TPU:1, one launch (start us, length us, event | category | flops | bytes accessed | tf_op | source)
XLA Modules:
  0.0 60.5 jit_solution(9738554538181513094)
XLA Ops:
  0.0 0.0 copy-start
  0.0 1.0 %copy-done = f32[16,48,128]{2,1,0:T(8,128)S(1)} copy-done((f32[16,48,128]{2,1,0:T(8,128)S(1)}, f32[16,48,128]{2,1,0:T(8,128)}, u32[]{:S(2)}) %copy-start) | copy-done | bytes 393240
  1.0 0.0 copy-start.1
  1.0 1.0 %copy-done.1 = f32[16,48,128]{2,1,0:T(8,128)S(1)} copy-done((f32[16,48,128]{2,1,0:T(8,128)S(1)}, f32[16,48,128]{2,1,0:T(8,128)}, u32[]{:S(2)}) %copy-start.1) | copy-done | bytes 393240
  2.0 0.0 copy-start.2
  2.0 1.0 %copy-done.2 = f32[16,48,128]{2,1,0:T(8,128)S(1)} copy-done((f32[16,48,128]{2,1,0:T(8,128)S(1)}, f32[16,48,128]{2,1,0:T(8,128)}, u32[]{:S(2)}) %copy-start.2) | copy-done | bytes 393240
  3.0 56.8 %shard_map.37 = f32[16,48,128]{2,1,0:T(8,128)S(1)} custom-call(f32[16,48,128]{2,1,0:T(8,128)S(1)} %copy-done, f32[16,48,128]{2,1,0:T(8,128)S(1)} %copy-done.1, f32[16,48,128]{2,1,0:T(8,128)S(1)} %copy-done.2), custom_call_target="tpu_custom_call" | custom-call | tf_op jit(solution)/shard_map/pallas_call | solution.py:644
  59.8 0.7 %copy.5 = f32[16,48,128]{2,1,0:T(8,128)} copy(f32[16,48,128]{2,1,0:T(8,128)S(1)} %shard_map.37) | data formatting | bytes 786432
Async XLA Ops:
  0.0 1.0 %copy-start = (f32[16,48,128]{2,1,0:T(8,128)S(1)}, f32[16,48,128]{2,1,0:T(8,128)}, u32[]{:S(2)}) copy-start(f32[16,48,128]{2,1,0:T(8,128)} %rhs.1) | copy-start | bytes 1179652
  1.0 1.0 %copy-start.1 = (f32[16,48,128]{2,1,0:T(8,128)S(1)}, f32[16,48,128]{2,1,0:T(8,128)}, u32[]{:S(2)}) copy-start(f32[16,48,128]{2,1,0:T(8,128)} %coef_b.1) | copy-start | bytes 1179652
  2.0 1.0 %copy-start.2 = (f32[16,48,128]{2,1,0:T(8,128)S(1)}, f32[16,48,128]{2,1,0:T(8,128)}, u32[]{:S(2)}) copy-start(f32[16,48,128]{2,1,0:T(8,128)} %coef_c.1) | copy-start | bytes 1179652

commit v5 on v4

--- a/solution.py
+++ b/solution.py
@@ -47,14 +47,21 @@
 WINDOW = (None, (16, 40), (16, 48), (8, 24))
 FIRST_ROW = (0, 8, 18, 9)
 NEAR = (-2, -1, 1, 2)
-TOGETHER = 8
+TOGETHER = 16
 
 
 def make_kernel(shape, sizes, plan):
     count = {axis: sizes[axis] for axis in AXES}
 
-    def kernel(rhs, coef_b, coef_c, out, *scratch):
+    def kernel(rhs_in, coef_b_in, coef_c_in, out, *scratch):
         refs = plan.unpack(scratch)
+        rhs, coef_c = refs.rhs, refs.coef_c
+        inputs = [
+            pltpu.make_async_copy(source, target, refs.load.at[i])
+            for i, (source, target) in enumerate((
+                (coef_b_in, refs.level[0].b.vp.at[pl.ds(1, shape[0]), pl.ds(PAD, shape[1])]),
+                (coef_c_in, coef_c), (rhs_in, rhs)))
+        ]
         place = {axis: lax.axis_index(axis) for axis in AXES}
 
         def beyond(axis, step):
@@ -79,7 +86,8 @@
         for offset in partners:
             pl.semaphore_signal(barrier, inc=1, device_id={a: beyond(a, d) for a, d in zip(AXES, offset)},
                                 device_id_type=MESH)
-        pl.semaphore_wait(barrier, len(partners))
+        for copy in inputs:
+            copy.start()
 
         lane = lax.broadcasted_iota(jnp.int32, (1, LANES), 1)
 
@@ -149,7 +157,7 @@
 
             lax.fori_loop(0, n // step, plain, 0)
 
-        def sweep(level, make, h):
+        def sweep(level, make, h, held=False):
             nx, ny = dims(level)
             nz = own(level)[2]
             def keep(x, plane):
@@ -161,7 +169,8 @@
             zero = jnp.zeros((ny, LANES), jnp.float32)
 
             def pack(x, plane, carry):
-                keep(x, plane)
+                if not held:
+                    keep(x, plane)
                 high, low = carry
                 h.ys[0, pl.ds(x, 1), :] = plane[ny - 1:ny]
                 h.ys[1, pl.ds(x, 1), :] = plane[0:1]
@@ -173,6 +182,8 @@
             high, low = planes(nx, make, pack, (zero, zero))
             h.zs[0, pl.ds(0, ny), :] = high
             h.zs[1, pl.ds(0, ny), :] = low
+            if held:
+                pl.semaphore_wait(barrier, len(partners))
             for copy in copies(level, h):
                 copy.start()
 
@@ -247,9 +258,11 @@
                 outer = jnp.where(high, pltpu.roll(plane, 8 * x + 8, 1), outer)
             h.outer[which] = outer
 
-        def part_copies(h, deep):
+        def part_copies(h, deep, steps=(1, 2, 3)):
             every = []
             for i, (dx, dy, dz) in enumerate(around_all):
+                if abs(dx) + abs(dy) + abs(dz) not in steps:
+                    continue
                 rows = {-1: pl.ds(0, 8), 0: pl.ds(0, own(1)[1]), 1: pl.ds(own(1)[1] - 8, 8)}[dy]
                 pairs = {-1: pl.ds(0, deep), 0: pl.ds(0, 4), 1: pl.ds(4 - deep, deep)}[dx]
                 every_array = slice(None)
@@ -264,8 +277,8 @@
                     device_id={a: beyond(a, d) for a, d in zip(AXES, (dx, dy, dz))}, device_id_type=MESH))
             return every
 
-        def parts_start(h, deep):
-            for copy in part_copies(h, deep):
+        def parts_start(h, deep, steps=(1, 2, 3)):
+            for copy in part_copies(h, deep, steps):
                 copy.start()
 
         def parts_end(h, deep):
@@ -444,21 +457,27 @@
 
         parts_f, parts_bc = refs.parts
         own_planes = own(0)[0]
-        sweep(0, lambda x: coef_b[x], levels[0].b)
-        made_b = coarsen(0, own_planes, lambda x: coef_b[x])
+        inputs[0].wait()
+        fine_b = planes_of(0, levels[0].b)
+        sweep(0, fine_b, levels[0].b, held=True)
+        made_b = coarsen(0, own_planes, fine_b)
+        inputs[1].wait()
         block_parts(parts_bc, 0, made_b)
         made_c = coarsen(0, own_planes, lambda x: coef_c[x])
         block_parts(parts_bc, 1, made_c)
+        parts_start(parts_bc, 3, (1,))
         for which, made in enumerate((made_b, made_c)):
             for x, plane in enumerate(made):
                 levels[1].e[x, pl.ds(0, own(1)[1]), :] = plane
             coarsen(1, own(1)[0], lambda x: levels[1].e[x, pl.ds(0, own(1)[1]), :], block_to(of_bc, which))
 
         setup(0)
+        inputs[2].wait()
         start_down(0)
         gather_near(of_bc)
+        parts_start(parts_bc, 3, (2,))
         go_down(0)
-        parts_start(parts_bc, 3)
+        parts_start(parts_bc, 3, (3,))
         gather_all(of_bc, 2)
 
         block_parts(parts_f, 0, leave(0))
@@ -592,6 +611,9 @@
                 g.pair = planes(nx // 2)
             g.it = [halo(exchanged) for _ in range(4 if exchanged else 2)]
             self.tree.level.append(g)
+        self.tree.rhs = self.add(pltpu.VMEM(shape, jnp.float32))
+        self.tree.coef_c = self.add(pltpu.VMEM(shape, jnp.float32))
+        self.tree.load = self.add(pltpu.SemaphoreType.DMA((3,)))
         self.tree.gather = [self.gathered(1), self.gathered(2)]
         self.tree.parts = [self.parted(1, shape[1] // 2), self.parted(2, shape[1] // 2)]
 
@@ -644,11 +666,11 @@
         return pl.pallas_call(
             make_kernel(shape, sizes, plan),
             out_shape=jax.ShapeDtypeStruct(shape, jnp.float32),
-            in_specs=[pl.BlockSpec(memory_space=pltpu.VMEM)] * 3,
+            in_specs=[pl.BlockSpec(memory_space=pl.ANY)] * 3,
             out_specs=pl.BlockSpec(memory_space=pltpu.VMEM),
             scratch_shapes=plan.shapes,
             compiler_params=pltpu.CompilerParams(
-                collective_id=0, has_side_effects=True, vmem_limit_bytes=40 * 2**20),
+                collective_id=0, has_side_effects=True, vmem_limit_bytes=56 * 2**20),
         )(rhs, coef_b, coef_c)
 
     return jax.shard_map(

time: 60.7 us -> 52.8 us (0.87)
  Pallas kernels: 56.8 us -> 50.9 us
  local copies, waits for them, and re-layouts: 3.73 us -> 1.77 us
    pallas_call x1, Pallas kernels: 56.8 us -> 50.9 us  [local(): pl.pallas_call(make_kernel(shape, sizes, plan), out_shape=jax.ShapeDtypeS...]
    unnamed x7 -> x1, local copies, waits for them, and re-layouts: 3.73 us -> 1.77 us
where the time goes in v5:
time: 52.8 us; the launch traced here: 52.7 us
  Pallas kernels  50.9 us (96%)
  local copies, waits for them, and re-layouts  1.77 us (3%)
    pallas_call x1, Pallas kernels, local(): pl.pallas_call(make_kernel(shape, sizes, plan), out_shape=jax.ShapeDtypeS...  50.9 us
    unnamed x1, local copies, waits for them, and re-layouts  1.77 us

profile of v5, /device:TPU:1, one launch (start us, length us, event | category | flops | bytes accessed | tf_op | source)
XLA Modules:
  0.0 52.7 jit_solution(1866061504289523291)
XLA Ops:
  0.0 50.9 %shard_map.37 = f32[16,48,128]{2,1,0:T(8,128)} custom-call(f32[16,48,128]{2,1,0:T(8,128)} %rhs_in.1, f32[16,48,128]{2,1,0:T(8,128)} %coef_b_in.1, f32[16,48,128]{2,1,0:T(8,128)} %coef_c_in.1), custom_call_target="tpu_custom_call" | custom-call | tf_op jit(solution)/shard_map/pallas_call | solution.py:666
  50.9 1.8 %copy.5 = f32[16,48,128]{2,1,0:T(8,128)} copy(f32[16,48,128]{2,1,0:T(8,128)} %shard_map.37) | data formatting | bytes 786432

commit v6 on v5

--- a/solution.py
+++ b/solution.py
@@ -34,14 +34,16 @@
     pass
 
 
-def exact_dot(left, matrix):
+def exact_dot(lefts, matrix):
+    left = jnp.concatenate(lefts, axis=0)
     high = left.astype(jnp.bfloat16)
     rest = left - high.astype(jnp.float32)
     middle = rest.astype(jnp.bfloat16)
     low = (rest - middle.astype(jnp.float32)).astype(jnp.bfloat16)
-    total = jnp.dot(low, matrix, preferred_element_type=jnp.float32)
-    total = total + jnp.dot(middle, matrix, preferred_element_type=jnp.float32)
-    return total + jnp.dot(high, matrix, preferred_element_type=jnp.float32)
+    product = jnp.dot(jnp.concatenate([low, middle, high], axis=0), matrix, preferred_element_type=jnp.float32)
+    total, rows = left.shape[0], lefts[0].shape[0]
+    product = (product[:total] + product[total:2 * total]) + product[2 * total:]
+    return [product[rows * k:rows * k + rows] for k in range(len(lefts))]
 
 
 WINDOW = (None, (16, 40), (16, 48), (8, 24))
@@ -110,14 +112,14 @@
         def copies(level, h):
             nx, ny = dims(level)
             rows = pl.ds(PAD, round_up(ny))
-            vp, zs, zr, ys, yr = h.vp, h.zs, h.zr, h.ys, h.yr
+            vp, zs, zin, ys, yr = h.vp, h.zs, h.zin, h.ys, h.yr
             pairs = (
                 (vp.at[nx, rows], vp.at[0, rows], "gx", after),
                 (vp.at[1, rows], vp.at[nx + 1, rows], "gx", before),
                 (ys.at[0], yr.at[0], "gy", after),
                 (ys.at[1], yr.at[1], "gy", before),
-                (zs.at[0], zr.at[0], "gz", after),
-                (zs.at[1], zr.at[1], "gz", before),
+                (zs.at[0], zin.at[0], "gz", after),
+                (zs.at[1], zin.at[1], "gz", before),
             )
             return [
                 pltpu.make_async_remote_copy(
@@ -132,6 +134,10 @@
             nx, ny = dims(level)
             for copy in copies(level, h):
                 copy.wait()
+            for side in range(2):
+                packed = h.zin[side]
+                for tile in range(ny // 8):
+                    h.zr[side, pl.ds(8 * tile, 8), :] = pltpu.roll(packed, (LANES - nx * tile) % LANES, 1)
             for x in range(nx):
                 h.vp[x + 1, pl.ds(PAD - 1, 1), :] = h.yr[0, pl.ds(x, 1), :]
                 h.vp[x + 1, pl.ds(PAD + ny, 1), :] = h.yr[1, pl.ds(x, 1), :]
@@ -180,8 +186,12 @@
                 return high, low
 
             high, low = planes(nx, make, pack, (zero, zero))
-            h.zs[0, pl.ds(0, ny), :] = high
-            h.zs[1, pl.ds(0, ny), :] = low
+            for side, columns in enumerate((high, low)):
+                packed = columns[0:8]
+                for tile in range(1, ny // 8):
+                    moved = pltpu.roll(columns[8 * tile:8 * tile + 8], nx * tile, 1)
+                    packed = jnp.where((lane >= nx * tile) & (lane < nx * tile + nx), moved, packed)
+                h.zs[side] = packed
             if held:
                 pl.semaphore_wait(barrier, len(partners))
             for copy in copies(level, h):
@@ -226,12 +236,9 @@
                 pair[x, pl.ds(0, plane.shape[0]), :] = plane
 
             planes(count_x // 2, lambda x: get(2 * x) + get(2 * x + 1), put_pair)
-            half = (own(1)[1] // 2) if level == 1 else dims(level)[1] // 2
-            made = []
-            for x in range(count_x // 2):
-                even = pair[x, pl.ds(0, half, 2), :]
-                odd = pair[x, pl.ds(1, half, 2), :]
-                made.append(exact_dot(even + odd, shrink))
+            half = 16 if level == 1 else dims(level)[1] // 2
+            made = exact_dot([pair[x, pl.ds(0, half, 2), :] + pair[x, pl.ds(1, half, 2), :]
+                              for x in range(count_x // 2)], shrink)
             if put is not None:
                 for x, plane in enumerate(made):
                     put(x, plane)
@@ -240,11 +247,10 @@
         def refine(level, count_x, get):
             pair = refs.level[level].pair
             grow = jnp.where(pairing(level, col_of, row_of), 1.0, 0.0).astype(jnp.bfloat16)
-            for x in range(count_x):
-                wide = exact_dot(get(x), grow)
-                rows = wide.shape[0]
-                pair[x, pl.ds(0, rows, 2), :] = wide
-                pair[x, pl.ds(1, rows, 2), :] = wide
+            rows = min(get(0).shape[0], pair.shape[1] // 2)
+            for x, wide in enumerate(exact_dot([get(x) for x in range(count_x)], grow)):
+                pair[x, pl.ds(0, rows, 2), :] = wide[:rows]
+                pair[x, pl.ds(1, rows, 2), :] = wide[:rows]
 
         def block_parts(h, which, made):
             rows = own(1)[1]
@@ -317,7 +323,7 @@
 
         def block_to(h, which):
             def put(x, plane):
-                mean = pltpu.roll(jnp.where(lane < 32, plane, 0.0), 32 * x, 1)
+                mean = pltpu.roll(jnp.where(lane < 32, plane[:12], 0.0), 32 * x, 1)
                 rows = pl.ds(0, 12)
                 h.block[which, rows, :] = mean if x == 0 else h.block[which, rows, :] + mean
 
@@ -478,10 +484,10 @@
         parts_start(parts_bc, 3, (2,))
         go_down(0)
         parts_start(parts_bc, 3, (3,))
-        gather_all(of_bc, 2)
 
         block_parts(parts_f, 0, leave(0))
         parts_start(parts_f, 2)
+        gather_all(of_bc, 2)
 
         parts_end(parts_bc, 3)
         for w in range(-1, 17):
@@ -489,20 +495,6 @@
             if 0 <= w < 16:
                 put_pieces(levels[1].c, w, 0, part_plane(parts_bc, 1, w))
         setup(1)
-        gather_end(of_bc)
-        for dx in range(4):
-            def spread(x, carry, dx=dx):
-                levels[2].b.vp[4 * x + dx + 1, pl.ds(PAD, 48), :] = gathered(of_bc, 0, x, dx)
-                levels[2].c[4 * x + dx] = gathered(of_bc, 1, x, dx)
-                return carry
-
-            lax.fori_loop(0, 4, spread, 0)
-        coarsen(2, 16, planes_of(2, levels[2].b), store(levels[3].f))
-        sweep(3, lambda x: levels[3].f[x], levels[3].b)
-        coarsen(2, 16, lambda x: levels[2].c[x], store(levels[3].c))
-        setup(2)
-        setup(3)
-
         parts_end(parts_f, 2)
         for w in range(16):
             put_pieces(levels[1].f, w, 0, part_plane(parts_f, 0, w))
@@ -511,6 +503,19 @@
         leave(1, block_to(of_f, 0))
         gather_near(of_f)
         gather_all(of_f, 1)
+        gather_end(of_bc)
+        for dx in range(4):
+            def spread(x, carry, dx=dx):
+                levels[2].b.vp[4 * x + dx + 1, pl.ds(PAD, 48), :] = gathered(of_bc, 0, x, dx)
+                levels[2].c[4 * x + dx] = gathered(of_bc, 1, x, dx)
+                return carry
+
+            lax.fori_loop(0, 4, spread, 0)
+        coarsen(2, 16, planes_of(2, levels[2].b), store(levels[3].f))
+        sweep(3, lambda x: levels[3].f[x], levels[3].b)
+        coarsen(2, 16, lambda x: levels[2].c[x], store(levels[3].c))
+        setup(2)
+        setup(3)
         gather_end(of_f)
         for dx in range(4):
             def spread_f(x, carry, dx=dx):
@@ -548,7 +553,7 @@
 
         g = levels[1]
         start_x = place["gx"] * own(2)[0] - 2
-        refine(1, 8, lambda x: levels[2].f[jnp.clip(start_x + x, 0, 15), pl.ds(14, 20), :])
+        refine(1, 8, lambda x: levels[2].f[jnp.clip(start_x + x, 0, 15), pl.ds(14, 24), :])
         sweep(1, lambda x: planes_of(1, g.it[1])(x) + g.pair[x // 2], g.it[0])
         go_up(1, g.it[0], g.it[1], store(g.f))
 
@@ -590,7 +595,7 @@
                 h = Names()
                 h.vp = self.add(pltpu.VMEM((nx + 2, round_up(ny) + 2 * PAD, LANES), jnp.float32))
                 if exchanged:
-                    for name, rows in (("zs", ny), ("zr", ny), ("ys", nx), ("yr", nx)):
+                    for name, rows in (("zs", 8), ("zin", 8), ("zr", ny), ("ys", nx), ("yr", nx)):
                         setattr(h, name, self.add(pltpu.VMEM((2, round_up(rows), LANES), jnp.float32)))
                     h.send = self.add(pltpu.SemaphoreType.DMA((6,)))
                     h.recv = self.add(pltpu.SemaphoreType.DMA((6,)))

time: 52.8 us -> 51 us (0.966)
  Pallas kernels: 50.9 us -> 49.1 us
    pallas_call x1, Pallas kernels: 50.9 us -> 49.1 us  [local(): pl.pallas_call(make_kernel(shape, sizes, plan), out_shape=jax.ShapeDtypeS...]
where the time goes in v6:
time: 51 us; the launch traced here: 50.9 us
  Pallas kernels  49.1 us (96%)
  local copies, waits for them, and re-layouts  1.77 us (3%)
    pallas_call x1, Pallas kernels, local(): pl.pallas_call(make_kernel(shape, sizes, plan), out_shape=jax.ShapeDtypeS...  49.1 us
    unnamed x1, local copies, waits for them, and re-layouts  1.77 us

profile of v6, /device:TPU:1, one launch (start us, length us, event | category | flops | bytes accessed | tf_op | source)
XLA Modules:
  0.0 50.9 jit_solution(3862739614004777869)
XLA Ops:
  0.0 49.1 %shard_map.37 = f32[16,48,128]{2,1,0:T(8,128)} custom-call(f32[16,48,128]{2,1,0:T(8,128)} %rhs_in.1, f32[16,48,128]{2,1,0:T(8,128)} %coef_b_in.1, f32[16,48,128]{2,1,0:T(8,128)} %coef_c_in.1), custom_call_target="tpu_custom_call" | custom-call | tf_op jit(solution)/shard_map/pallas_call | solution.py:671
  49.1 1.8 %copy.5 = f32[16,48,128]{2,1,0:T(8,128)} copy(f32[16,48,128]{2,1,0:T(8,128)} %shard_map.37) | data formatting | bytes 786432

commit v7 on v6

--- a/solution.py
+++ b/solution.py
@@ -321,6 +321,9 @@
 
             return put
 
+        levels = refs.level
+        of_f, of_bc = refs.gather
+
         def block_to(h, which):
             def put(x, plane):
                 mean = pltpu.roll(jnp.where(lane < 32, plane[:12], 0.0), 32 * x, 1)
@@ -338,13 +341,15 @@
             ]
 
         def all_copies(h):
-            return [
-                pltpu.make_async_remote_copy(
-                    src_ref=h.column, dst_ref=h.all.at[1 - dz, place["gx"]], send_sem=h.all_send.at[1 - dz, dx],
-                    recv_sem=h.all_recv.at[1 - dz, dx],
-                    device_id={"gx": beyond("gx", dx), "gz": beyond("gz", dz)}, device_id_type=MESH)
-                for dx, dz in around_xz
-            ]
+            every = []
+            for dx, dz in around_xz:
+                src, dst = h.column, h.all.at[1 - dz, place["gx"]]
+                if dz and h is of_f:
+                    src, dst = h.halves.at[(1 + dz) // 2], h.side.at[(1 - dz) // 2, place["gx"]]
+                every.append(pltpu.make_async_remote_copy(
+                    src_ref=src, dst_ref=dst, send_sem=h.all_send.at[1 - dz, dx], recv_sem=h.all_recv.at[1 - dz, dx],
+                    device_id={"gx": beyond("gx", dx), "gz": beyond("gz", dz)}, device_id_type=MESH))
+            return every
 
         def gather_near(h):
             for copy in near_copies(h):
@@ -359,6 +364,11 @@
                 h.column[k, pl.ds(18, 12), :] = h.block[k, pl.ds(0, 12), :]
                 h.column[k, pl.ds(30, 12), :] = h.near[2, k, pl.ds(0, 12), :]
                 h.column[k, pl.ds(42, 6), :] = h.near[3, k, pl.ds(0, 6), :]
+            if h is of_f:
+                lower = lax.rem(lane, 32) < 16
+                top, bottom = h.column[0, pl.ds(0, 24), :], h.column[0, pl.ds(24, 24), :]
+                h.halves[0] = jnp.where(lower, top, pltpu.roll(bottom, 16, 1))
+                h.halves[1] = jnp.where(lower, pltpu.roll(bottom, LANES - 16, 1), top)
             for copy in all_copies(h):
                 copy.start()
             h.all[1, place["gx"]] = h.column[...]
@@ -368,6 +378,17 @@
                 copy.wait()
 
         def gathered(h, which, x, dx):
+            if h is of_f:
+                here = h.all[1, x, which]
+                left, right = h.side[0, x], h.side[1, x]
+                plane = jnp.where(lane < 32, pltpu.roll(here, (LANES - 32 * dx) % LANES, 1), 0.0)
+                parts = []
+                for k, part in enumerate((plane[:24], plane[24:])):
+                    moved = pltpu.roll(right, (LANES + 32 - 16 * k - 32 * dx) % LANES, 1)
+                    part = jnp.where((lane >= 32) & (lane < 48), moved, part)
+                    moved = pltpu.roll(left, (LANES + 96 + 16 * k - 32 * dx) % LANES, 1)
+                    parts.append(jnp.where(lane >= 112, moved, part))
+                return jnp.concatenate(parts, axis=0)
             left, here, right = (h.all[i, x, which] for i in range(3))
             plane = jnp.where(lane < 32, pltpu.roll(here, (LANES - 32 * dx) % LANES, 1), 0.0)
             plane = jnp.where((lane >= 32) & (lane < 64), pltpu.roll(right, (LANES + 32 - 32 * dx) % LANES, 1), plane)
@@ -417,9 +438,7 @@
             ny = dims(level)[1]
             return lambda x: h.vp[x + 1, pl.ds(PAD, ny), :]
 
-        levels = refs.level
         (_, first), (carry_e, weight_r) = chebyshev(2)
-        of_f, of_bc = refs.gather
 
         def start_down(level):
             g = levels[level]
@@ -505,12 +524,9 @@
         gather_all(of_f, 1)
         gather_end(of_bc)
         for dx in range(4):
-            def spread(x, carry, dx=dx):
+            for x in range(4):
                 levels[2].b.vp[4 * x + dx + 1, pl.ds(PAD, 48), :] = gathered(of_bc, 0, x, dx)
                 levels[2].c[4 * x + dx] = gathered(of_bc, 1, x, dx)
-                return carry
-
-            lax.fori_loop(0, 4, spread, 0)
         coarsen(2, 16, planes_of(2, levels[2].b), store(levels[3].f))
         sweep(3, lambda x: levels[3].f[x], levels[3].b)
         coarsen(2, 16, lambda x: levels[2].c[x], store(levels[3].c))
@@ -518,11 +534,8 @@
         setup(3)
         gather_end(of_f)
         for dx in range(4):
-            def spread_f(x, carry, dx=dx):
+            for x in range(4):
                 levels[2].f[4 * x + dx] = gathered(of_f, 0, x, dx)
-                return carry
-
-            lax.fori_loop(0, 4, spread_f, 0)
 
         start_down(2)
         go_down(2)
@@ -638,6 +651,9 @@
         h.near = self.add(pltpu.VMEM((4, arrays, 16, LANES), jnp.float32))
         h.column = self.add(pltpu.VMEM((arrays, 48, LANES), jnp.float32))
         h.all = self.add(pltpu.VMEM((3, 4, arrays, 48, LANES), jnp.float32))
+        if arrays == 1:
+            h.halves = self.add(pltpu.VMEM((2, 24, LANES), jnp.float32))
+            h.side = self.add(pltpu.VMEM((2, 4, 24, LANES), jnp.float32))
         h.near_send = self.add(pltpu.SemaphoreType.DMA((4,)))
         h.near_recv = self.add(pltpu.SemaphoreType.DMA((4,)))
         h.all_send = self.add(pltpu.SemaphoreType.DMA((3, 4)))

time: 51 us -> 49.5 us (0.971)
  Pallas kernels: 49.1 us -> 47.5 us
    pallas_call x1, Pallas kernels: 49.1 us -> 47.5 us  [local(): pl.pallas_call(make_kernel(shape, sizes, plan), out_shape=jax.ShapeDtypeS...]
where the time goes in v7:
time: 49.5 us; the launch traced here: 49.3 us
  Pallas kernels  47.5 us (96%)
  local copies, waits for them, and re-layouts  1.77 us (4%)
    pallas_call x1, Pallas kernels, local(): pl.pallas_call(make_kernel(shape, sizes, plan), out_shape=jax.ShapeDtypeS...  47.5 us
    unnamed x1, local copies, waits for them, and re-layouts  1.77 us

profile of v7, /device:TPU:1, one launch (start us, length us, event | category | flops | bytes accessed | tf_op | source)
XLA Modules:
  0.0 49.3 jit_solution(17594177401624353800)
XLA Ops:
  0.0 47.5 %shard_map.37 = f32[16,48,128]{2,1,0:T(8,128)} custom-call(f32[16,48,128]{2,1,0:T(8,128)} %rhs_in.1, f32[16,48,128]{2,1,0:T(8,128)} %coef_b_in.1, f32[16,48,128]{2,1,0:T(8,128)} %coef_c_in.1), custom_call_target="tpu_custom_call" | custom-call | tf_op jit(solution)/shard_map/pallas_call | solution.py:687
  47.6 1.8 %copy.5 = f32[16,48,128]{2,1,0:T(8,128)} copy(f32[16,48,128]{2,1,0:T(8,128)} %shard_map.37) | data formatting | bytes 786432

commit v8 on v7

--- a/solution.py
+++ b/solution.py
@@ -691,7 +691,7 @@
             out_specs=pl.BlockSpec(memory_space=pltpu.VMEM),
             scratch_shapes=plan.shapes,
             compiler_params=pltpu.CompilerParams(
-                collective_id=0, has_side_effects=True, vmem_limit_bytes=56 * 2**20),
+                collective_id=0, has_side_effects=True, vmem_limit_bytes=40 * 2**20),
         )(rhs, coef_b, coef_c)
 
     return jax.shard_map(

time: 49.5 us -> 50.8 us (1.026)
  local copies, waits for them, and re-layouts: 1.77 us -> 3.73 us
  Pallas kernels: 47.5 us -> 46.9 us
    unnamed x1 -> x7, local copies, waits for them, and re-layouts: 1.77 us -> 3.73 us
    pallas_call x1, Pallas kernels: 47.5 us -> 46.9 us  [local(): pl.pallas_call(make_kernel(shape, sizes, plan), out_shape=jax.ShapeDtypeS...]
where the time goes in v8:
time: 50.8 us; the launch traced here: 50.6 us
  Pallas kernels  46.9 us (92%)
  local copies, waits for them, and re-layouts  3.73 us (7%)
    pallas_call x1, Pallas kernels, local(): pl.pallas_call(make_kernel(shape, sizes, plan), out_shape=jax.ShapeDtypeS...  46.9 us
    unnamed x7, local copies, waits for them, and re-layouts  3.73 us

profile of v8, /device:TPU:1, one launch (start us, length us, event | category | flops | bytes accessed | tf_op | source)
XLA Modules:
  0.0 50.6 jit_solution(13697174433589121257)
XLA Ops:
  0.0 0.0 copy-start
  0.0 1.0 %copy-done = f32[16,48,128]{2,1,0:T(8,128)S(1)} copy-done((f32[16,48,128]{2,1,0:T(8,128)S(1)}, f32[16,48,128]{2,1,0:T(8,128)}, u32[]{:S(2)}) %copy-start) | copy-done | bytes 393240
  1.0 0.0 copy-start.1
  1.0 1.0 %copy-done.1 = f32[16,48,128]{2,1,0:T(8,128)S(1)} copy-done((f32[16,48,128]{2,1,0:T(8,128)S(1)}, f32[16,48,128]{2,1,0:T(8,128)}, u32[]{:S(2)}) %copy-start.1) | copy-done | bytes 393240
  2.0 0.0 copy-start.2
  2.0 1.0 %copy-done.2 = f32[16,48,128]{2,1,0:T(8,128)S(1)} copy-done((f32[16,48,128]{2,1,0:T(8,128)S(1)}, f32[16,48,128]{2,1,0:T(8,128)}, u32[]{:S(2)}) %copy-start.2) | copy-done | bytes 393240
  3.0 46.9 %shard_map.37 = f32[16,48,128]{2,1,0:T(8,128)S(1)} custom-call(f32[16,48,128]{2,1,0:T(8,128)S(1)} %copy-done, f32[16,48,128]{2,1,0:T(8,128)S(1)} %copy-done.1, f32[16,48,128]{2,1,0:T(8,128)S(1)} %copy-done.2), custom_call_target="tpu_custom_call" | custom-call | tf_op jit(solution)/shard_map/pallas_call | solution.py:687
  49.8 0.7 %copy.5 = f32[16,48,128]{2,1,0:T(8,128)} copy(f32[16,48,128]{2,1,0:T(8,128)S(1)} %shard_map.37) | data formatting | bytes 786432
Async XLA Ops:
  0.0 1.0 %copy-start = (f32[16,48,128]{2,1,0:T(8,128)S(1)}, f32[16,48,128]{2,1,0:T(8,128)}, u32[]{:S(2)}) copy-start(f32[16,48,128]{2,1,0:T(8,128)} %rhs_in.1) | copy-start | bytes 1179652
  1.0 1.0 %copy-start.1 = (f32[16,48,128]{2,1,0:T(8,128)S(1)}, f32[16,48,128]{2,1,0:T(8,128)}, u32[]{:S(2)}) copy-start(f32[16,48,128]{2,1,0:T(8,128)} %coef_b_in.1) | copy-start | bytes 1179652
  2.0 1.0 %copy-start.2 = (f32[16,48,128]{2,1,0:T(8,128)S(1)}, f32[16,48,128]{2,1,0:T(8,128)}, u32[]{:S(2)}) copy-start(f32[16,48,128]{2,1,0:T(8,128)} %coef_c_in.1) | copy-start | bytes 1179652

commit v9 on v7

--- a/solution.py
+++ b/solution.py
@@ -506,7 +506,6 @@
 
         block_parts(parts_f, 0, leave(0))
         parts_start(parts_f, 2)
-        gather_all(of_bc, 2)
 
         parts_end(parts_bc, 3)
         for w in range(-1, 17):
@@ -514,6 +513,7 @@
             if 0 <= w < 16:
                 put_pieces(levels[1].c, w, 0, part_plane(parts_bc, 1, w))
         setup(1)
+        gather_all(of_bc, 2)
         parts_end(parts_f, 2)
         for w in range(16):
             put_pieces(levels[1].f, w, 0, part_plane(parts_f, 0, w))

time: 49.5 us -> 50.1 us (1.012)
  Pallas kernels: 47.5 us -> 48.2 us
    pallas_call x1, Pallas kernels: 47.5 us -> 48.2 us  [local(): pl.pallas_call(make_kernel(shape, sizes, plan), out_shape=jax.ShapeDtypeS...]
where the time goes in v9:
time: 50.1 us; the launch traced here: 49.9 us
  Pallas kernels  48.2 us (96%)
  local copies, waits for them, and re-layouts  1.77 us (4%)
    pallas_call x1, Pallas kernels, local(): pl.pallas_call(make_kernel(shape, sizes, plan), out_shape=jax.ShapeDtypeS...  48.2 us
    unnamed x1, local copies, waits for them, and re-layouts  1.77 us

profile of v9, /device:TPU:1, one launch (start us, length us, event | category | flops | bytes accessed | tf_op | source)
XLA Modules:
  0.0 49.9 jit_solution(17839667267174363698)
XLA Ops:
  0.0 48.2 %shard_map.37 = f32[16,48,128]{2,1,0:T(8,128)} custom-call(f32[16,48,128]{2,1,0:T(8,128)} %rhs_in.1, f32[16,48,128]{2,1,0:T(8,128)} %coef_b_in.1, f32[16,48,128]{2,1,0:T(8,128)} %coef_c_in.1), custom_call_target="tpu_custom_call" | custom-call | tf_op jit(solution)/shard_map/pallas_call | solution.py:687
  48.2 1.8 %copy.5 = f32[16,48,128]{2,1,0:T(8,128)} copy(f32[16,48,128]{2,1,0:T(8,128)} %shard_map.37) | data formatting | bytes 786432
